TPU v7x, 128 devices: a whole 4x4x4 slice. The times are simulated.
128 devices in a mesh: rep: 16 (over y_hi, x, core), shard: 8 (over z, y_lo).
Axes of the slice: x: 4, y: 4 (y_hi: 2, y_lo: 2; y = y_hi * 2 + y_lo), z: 4, core: 2. Of those that a mesh axis runs over, the one named last changes fastest.
Arguments:
- tokens: bfloat16 [16, 1024, 1024], P('rep', 'shard'), may hold values from -6 to 6
- input_weight: bfloat16 [1024, 3072], P('shard'), may hold values from -0.1875 to 0.1875
- query_value_bias: bfloat16 [2048], P('shard'), may hold values from -3 to 3
- output_weight: bfloat16 [1024, 1024], P('shard'), may hold values from -4 to 4
- output_bias: bfloat16 [1024], P('shard'), may hold values from -3 to 3
- expand_weight: bfloat16 [1024, 4096], P('shard'), may hold values from -0.1875 to 0.1875
- expand_bias: bfloat16 [4096], P('shard'), may hold values from -3 to 3
- reduce_weight: bfloat16 [4096, 1024], P('shard'), may hold values from -0.09375 to 0.09375
- reduce_bias: bfloat16 [1024], P('shard'), may hold values from -3 to 3
- first_gain: bfloat16 [1024], P('shard'), may hold values from 0.5 to 1.5
- first_shift: bfloat16 [1024], P('shard'), may hold values from -3 to 3
- second_gain: bfloat16 [1024], P('shard'), may hold values from 0.5 to 1.5
- second_shift: bfloat16 [1024], P('shard'), may hold values from -3 to 3
- attention_scale: bfloat16 [1024], P('shard'), may hold values from 0.5 to 2
- feedforward_scale: bfloat16 [1024], P('shard'), may hold values from 0.5 to 2
- cotangent: bfloat16 [16, 1024, 1024], P('rep', 'shard'), may hold values from -6 to 6
Outputs:
- layer_output: bfloat16 [16, 1024, 1024], P('rep', 'shard')
- tokens_adjoint: bfloat16 [16, 1024, 1024], P('rep', 'shard')
- input_weight_adjoint: float32 [1024, 3072], P('shard')
- query_value_bias_adjoint: float32 [2048], P('shard')
- output_weight_adjoint: float32 [1024, 1024], P('shard')
- output_bias_adjoint: float32 [1024], P('shard')
- expand_weight_adjoint: float32 [1024, 4096], P('shard')
- expand_bias_adjoint: float32 [4096], P('shard')
- reduce_weight_adjoint: float32 [4096, 1024], P('shard')
- reduce_bias_adjoint: float32 [1024], P('shard')
- first_gain_adjoint: float32 [1024], P('shard')
- first_shift_adjoint: float32 [1024], P('shard')
- second_gain_adjoint: float32 [1024], P('shard')
- second_shift_adjoint: float32 [1024], P('shard')
- attention_scale_adjoint: float32 [1024], P('shard')
- feedforward_scale_adjoint: float32 [1024], P('shard')
All inputs are finite; a program needn't handle non-finite values.
Results may differ from a plain program's by a relative error of at most 0.024.
Values may be sent and summed in bfloat16 or wider, within the bound.
No kernel may reach another device: no remote copies, remote signals or barrier semaphores. Data moves between devices by JAX's collectives and lax.ppermute only.
A program may use at most 128 MiB of HBM per device.

v0:
```python
import functools

import jax
import jax.numpy as jnp
from jax import lax
from jax.experimental import pallas as pl
from jax.experimental.pallas import tpu as pltpu
from jax.sharding import Mesh, PartitionSpec as P

HEAD_DIM = 64
EPSILON = 1e-06
SHARD = ("z", "yl")
REP = ("yh", "x", "core")
NZ, NX = 4, 4
f32 = jnp.float32
bf16 = jnp.bfloat16


def normalised(values):
    mean = jnp.mean(values, axis=-1, keepdims=True)
    centred = values - mean
    variance = jnp.mean(centred * centred, axis=-1, keepdims=True)
    return centred * lax.rsqrt(variance + EPSILON)


def layer_norm(values, gain, shift):
    return normalised(values) * gain + shift


def exact_gelu(values):
    return jax.nn.gelu(values, approximate=False)


def times(left, right):
    return jnp.dot(left, right, preferred_element_type=f32)


def against(left, right):
    return lax.dot_general(left, right, (((1,), (1,)), ((), ())), preferred_element_type=f32)


def across(left, right):
    return lax.dot_general(left, right, (((0,), (0,)), ((), ())), preferred_element_type=f32)


SWAP = [(0, 1), (1, 0)]


def swap(block, axis):
    return lax.ppermute(block, axis, SWAP)


def trade(parts, axes):
    return lax.all_to_all(parts, axes, split_axis=0, concat_axis=0, tiled=True)


def gather(block, axes, n):
    return trade(jnp.broadcast_to(block[None], (n, *block.shape)), axes)


def pick(array, index, axis=0):
    return lax.dynamic_index_in_dim(array, index, axis, keepdims=False)


def both_cores(half, axis):
    other = swap(half, "core")
    first = lax.axis_index("core") == 0
    return jnp.concatenate([jnp.where(first, half, other), jnp.where(first, other, half)], axis=axis)


def ahead(block, axis, n, k):
    return lax.ppermute(block, axis, [((i + k) % n, i) for i in range(n)])


def give(block, axis, n, k):
    return lax.ppermute(block, axis, [(i, (i + k) % n) for i in range(n)])


def gather_x(block):
    return jnp.concatenate([block] + [ahead(block, "x", NX, k) for k in range(1, NX)], axis=0)


def return_x(parts):
    sent = [give(parts[k], "x", NX, k) for k in range(1, NX)]
    return parts[0].astype(f32) + sum(p.astype(f32) for p in sent)


def gather_column(block, other):
    low = lax.axis_index("yl") == 0
    column = jnp.stack([jnp.where(low, block, other), jnp.where(low, other, block)])
    return [column] + [ahead(column, "z", NZ, k) for k in range(1, NZ)]


def send_z(parts):
    z = lax.axis_index("z")
    return [pick(parts, z)] + [give(pick(parts, (z + k) % NZ), "z", NZ, k) for k in range(1, NZ)]


def arrivals(block):
    blocks = [block] + [ahead(block, "x", NX, k) for k in range(1, NX)]
    return blocks + [swap(b, "core") for b in blocks]


def place(vector, offset, shape):
    row, column = divmod(offset, shape[1])
    size = vector.shape[0]
    return jnp.pad(vector.reshape(1, size), ((row, shape[0] - row - 1), (column, shape[1] - column - size)))


def after_that(value, earlier):
    return lax.optimization_barrier((value, earlier))[0]


def total(parts):
    return jnp.sum(parts.astype(f32), axis=0)


VMEM = pl.BlockSpec(memory_space=pltpu.VMEM)


def assemble_kernel(place_ref, *refs):
    columns, outs = refs[:-3], refs[-3:]
    z, core = place_ref[0], place_ref[1]
    half = columns[0].shape[1] // 3
    for j, column in enumerate(columns):
        block, side = j % NZ, core if j < NZ else 1 - core
        for y in range(2):
            first = ((lax.rem(z + block, NZ) * 2 + y) * 2 + side) * half
            rows = pl.ds(pl.multiple_of(first, half), half)
            for out, at in zip(outs, range(0, 3 * half, half)):
                out[rows, :] = column[y, at : at + half, :]


def assemble(columns, z, core, width):
    whole = jax.ShapeDtypeStruct((width, width), bf16)
    return pl.pallas_call(
        assemble_kernel,
        out_shape=(whole, whole, whole),
        in_specs=[pl.BlockSpec(memory_space=pltpu.SMEM)] + [VMEM] * len(columns),
        out_specs=(VMEM, VMEM, VMEM),
        compiler_params=pltpu.CompilerParams(vmem_limit_bytes=32 * 2**20),
        cost_estimate=pl.CostEstimate(flops=0, bytes_accessed=12 * width * width, transcendentals=0),
    )(jnp.stack([z, core]).astype(jnp.int32), *columns)


def finish_kernel(place_ref, *refs):
    pieces, (in_ref, out_ref, vector_ref, scratch) = refs[:-4], refs[-4:]
    x, core = place_ref[0], place_ref[1]
    piece, width, part = pieces[0].shape[0], out_ref.shape[1], scratch.shape[1]
    for j, ref in enumerate(pieces):
        side = core if j < NX else 1 - core
        first = (side * NX + lax.rem(x + j % NX, NX)) * piece
        rows = pl.ds(pl.multiple_of(first, piece), piece)
        in_ref[rows, :] = ref[:, : 3 * width].astype(f32)
        scratch[rows, :] = ref[:, 3 * width : 3 * width + part].astype(f32)
        out_ref[rows, :] = ref[:, 3 * width + part :].astype(f32)
    vector_ref[...] = scratch[...].T


def finish(pieces, x, core, part, width):
    return pl.pallas_call(
        finish_kernel,
        out_shape=(
            jax.ShapeDtypeStruct((part, 3 * width), f32),
            jax.ShapeDtypeStruct((part, width), f32),
            jax.ShapeDtypeStruct((part, part), f32),
        ),
        in_specs=[pl.BlockSpec(memory_space=pltpu.SMEM)] + [VMEM] * len(pieces),
        out_specs=(VMEM, VMEM, VMEM),
        scratch_shapes=[pltpu.VMEM((part, part), f32)],
        compiler_params=pltpu.CompilerParams(vmem_limit_bytes=16 * 2**20),
        cost_estimate=pl.CostEstimate(flops=0, bytes_accessed=24 * part * width, transcendentals=0),
    )(jnp.stack([x, core]).astype(jnp.int32), *pieces)


def finish_pair_kernel(place_ref, *refs):
    pieces, (down_ref, up_ref) = refs[:-2], refs[-2:]
    x, core = place_ref[0], place_ref[1]
    part, width = pieces[0].shape
    half = part // 2
    for j, ref in enumerate(pieces):
        side = core if j < NX else 1 - core
        chip = lax.rem(x + j % NX, NX)
        first = (chip * 2 + side) * half
        down_ref[pl.ds(pl.multiple_of(first, half), half), :] = ref[:half, :].astype(f32)
        rows = pl.ds(pl.multiple_of(side * half, half), half)
        for s in range(width // part):
            at = pl.multiple_of((s * NX + chip) * part, part)
            up_ref[rows, pl.ds(at, part)] = ref[half:, s * part : (s + 1) * part].astype(f32)


def finish_pair(pieces, x, core, part, width):
    return pl.pallas_call(
        finish_pair_kernel,
        out_shape=(
            jax.ShapeDtypeStruct((NX * part, width), f32),
            jax.ShapeDtypeStruct((part, NX * width), f32),
        ),
        in_specs=[pl.BlockSpec(memory_space=pltpu.SMEM)] + [VMEM] * len(pieces),
        out_specs=(VMEM, VMEM),
        compiler_params=pltpu.CompilerParams(vmem_limit_bytes=16 * 2**20),
        cost_estimate=pl.CostEstimate(flops=0, bytes_accessed=48 * part * width, transcendentals=0),
    )(jnp.stack([x, core]).astype(jnp.int32), *pieces)


BLOCK = 256


def head_parts(mixed_ref, head, part):
    return [
        mixed_ref[:, j * part + head * HEAD_DIM : j * part + (head + 1) * HEAD_DIM] for j in range(3)
    ]


def forward_kernel(scaling, mixed_ref, attended_ref, lse_ref):
    length, part = attended_ref.shape
    for head in range(part // HEAD_DIM):
        query, key, value = head_parts(mixed_ref, head, part)
        query = query * jnp.asarray(scaling, bf16)
        value_t = value.T
        for at in range(0, length, BLOCK):
            scores = against(key, query[at : at + BLOCK])
            most = jnp.max(scores, axis=0, keepdims=True)
            weights = jnp.exp(scores - most)
            count = jnp.sum(weights, axis=0, keepdims=True)
            probs = (weights * (1.0 / count)).astype(bf16)
            attended_ref[at : at + BLOCK, head * HEAD_DIM : (head + 1) * HEAD_DIM] = (
                times(value_t, probs).T.astype(bf16)
            )
            lse_ref[head : head + 1, at : at + BLOCK] = most + jnp.log(count)


def backward_kernel(scaling, mixed_ref, lse_ref, grad_ref, out_ref):
    length, part = grad_ref.shape
    for head in range(part // HEAD_DIM):
        query, key, value = head_parts(mixed_ref, head, part)
        query = query * jnp.asarray(scaling, bf16)
        key_t = key.T
        columns = slice(head * HEAD_DIM, (head + 1) * HEAD_DIM)
        key_adj = jnp.zeros((length, HEAD_DIM), f32)
        value_adj = jnp.zeros((length, HEAD_DIM), f32)
        for at in range(0, length, BLOCK):
            rows = slice(at, at + BLOCK)
            grad = grad_ref[rows, columns]
            scores = against(key, query[rows])
            weights = jnp.exp(scores - lse_ref[head : head + 1, rows])
            prob_adj = against(value, grad)
            delta = jnp.sum(weights * prob_adj, axis=0, keepdims=True)
            score_adj = (weights * (prob_adj - delta)).astype(bf16)
            key_adj += times(score_adj, query[rows])
            value_adj += times(weights.astype(bf16), grad)
            out_ref[rows, columns] = (times(key_t, score_adj) * scaling).T.astype(bf16)
        out_ref[:, part + columns.start : part + columns.stop] = key_adj.astype(bf16)
        out_ref[:, 2 * part + columns.start : 2 * part + columns.stop] = value_adj.astype(bf16)


def attend_forward(mixed, scaling):
    length, part = mixed.shape[0], mixed.shape[1] // 3
    pairs = part * length * length
    return pl.pallas_call(
        functools.partial(forward_kernel, scaling),
        out_shape=(
            jax.ShapeDtypeStruct((length, part), bf16),
            jax.ShapeDtypeStruct((8, length), f32),
        ),
        compiler_params=pltpu.CompilerParams(vmem_limit_bytes=40 * 2**20),
        cost_estimate=pl.CostEstimate(
            flops=16 * pairs, bytes_accessed=8 * part * length, transcendentals=pairs // HEAD_DIM
        ),
    )(mixed)


def attend_backward(mixed, lse, grad, scaling):
    length, part = grad.shape
    pairs = part * length * length
    return pl.pallas_call(
        functools.partial(backward_kernel, scaling),
        out_shape=jax.ShapeDtypeStruct(mixed.shape, bf16),
        compiler_params=pltpu.CompilerParams(vmem_limit_bytes=40 * 2**20),
        cost_estimate=pl.CostEstimate(
            flops=40 * pairs, bytes_accessed=16 * part * length, transcendentals=pairs // HEAD_DIM
        ),
    )(mixed, lse, grad)


def shards(
    tokens,
    input_weight,
    query_value_bias,
    output_weight,
    output_bias,
    expand_weight,
    expand_bias,
    reduce_weight,
    reduce_bias,
    first_gain,
    first_shift,
    second_gain,
    second_shift,
    attention_scale,
    feedforward_scale,
    cotangent,
):
    _, rows, width = tokens.shape
    units = reduce_weight.shape[0]
    part = output_weight.shape[0]
    group = 8
    length = group * rows
    half = part // 2
    scaling = HEAD_DIM ** (-0.5)
    me = lax.axis_index("z") * 2 + lax.axis_index("yl")
    x, core = lax.axis_index("x"), lax.axis_index("core")

    own = tokens[0]
    extra = 8
    offset, small = 0, 0
    for vector in (
        query_value_bias,
        output_bias,
        reduce_bias,
        first_gain,
        first_shift,
        second_gain,
        second_shift,
        attention_scale,
        feedforward_scale,
        expand_bias,
    ):
        small = small + place(vector, offset, (extra, width))
        offset += vector.shape[0]
    band = part // 8
    w = input_weight.reshape(8, band, 3, group, part).transpose(3, 2, 1, 0, 4).reshape(group, 3 * band, width)
    here = jnp.concatenate([own, small], axis=0)
    blocks = jnp.concatenate([jnp.broadcast_to(here[None], (group, *here.shape)), w], axis=1)

    up_half = lax.dynamic_slice_in_dim(expand_weight, core * half, half, 0)
    up_half = pick(up_half.reshape(half, group, NX, part), x, 2).reshape(half, width)
    down_half = lax.dynamic_slice_in_dim(reduce_weight, x * part + core * half, half, 0)
    out_half = lax.dynamic_slice_in_dim(output_weight, core * half, half, 0)
    w = jnp.concatenate([up_half, down_half, out_half], axis=0)
    blocks, other = lax.optimization_barrier((blocks, swap(w, "yl")))
    columns = gather_column(w, other)
    upstreams = gather_x(cotangent[0]).astype(f32)

    blocks = trade(blocks, SHARD)
    all_tokens = blocks[:, :rows].reshape(length, width).astype(f32)
    smalls = blocks[:, rows : rows + 2].reshape(group, 2 * width).astype(f32)
    in_w = blocks[:, rows + extra :].reshape(group, 3, band, 8, part).transpose(0, 3, 2, 1, 4)
    in_w = in_w.reshape(width, 3 * part)
    pair_bias = smalls[:, : 2 * part].reshape(2 * width)
    out_bias, down_bias, gain_one, shift_one, gain_two, shift_two, scale_one, scale_two = [
        smalls[:, (2 + j) * part : (3 + j) * part].reshape(width) for j in range(8)
    ]
    at = 10 * part
    up_bias = pick(smalls[:, at : at + units].reshape(group, NX, part), x, 1).reshape(width)
    bias = jnp.concatenate(
        [
            lax.dynamic_slice(pair_bias, (me * part,), (part,)),
            jnp.zeros((part,), f32),
            lax.dynamic_slice(pair_bias, (width + me * part,), (part,)),
        ]
    )

    local = own.astype(f32)
    normal_one = normalised(all_tokens)
    hidden = (normal_one * gain_one + shift_one).astype(bf16)
    mixed = (times(hidden, in_w) + bias).astype(bf16)
    attended, lse = attend_forward(mixed, scaling)
    columns = [after_that(c, attended) for c in columns]
    columns = columns + [swap(c, "core") for c in columns]
    up_w, down_w, out_w = assemble(columns, lax.axis_index("z"), core, width)
    attended = trade(attended.reshape(group, rows, part), SHARD)
    attended = attended.transpose(1, 0, 2).reshape(rows, width)
    branch = times(attended, out_w) + out_bias
    after = local + scale_one * branch

    second_own = layer_norm(after, gain_two, shift_two).astype(bf16)
    second = gather_x(second_own)
    down_adj = (scale_two * upstreams).astype(bf16)

    pre = times(second, up_w) + up_bias
    act, gelu_pull = jax.vjp(exact_gelu, pre)
    act = act.astype(bf16)
    pre_adj = gelu_pull(against(down_adj, down_w))[0].astype(bf16)
    second_adj = return_x(against(pre_adj, up_w).astype(bf16).reshape(NX, rows, width))

    def add(mine, other, axis):
        return (mine.astype(f32) + swap(other.astype(bf16), axis).astype(f32)).astype(bf16)

    def core_sum(array):
        return add(pick(array, core, 1), pick(array, 1 - core, 1), "core")

    pair = jnp.stack(
        [
            core_sum(g.astype(bf16).reshape(group, 2, half, width))
            for g in (across(act, down_adj), across(second, pre_adj))
        ],
        axis=1,
    )
    second_adj = after_that(second_adj, pair)
    down_part = times(act, down_w)
    arrived = send_z(pair.reshape(NZ, 2, part, width))

    upstream = cotangent[0].astype(f32)
    _, norm_pull = jax.vjp(layer_norm, after, gain_two, shift_two)
    after_inner, gain_two_adj, shift_two_adj = norm_pull(second_adj)
    after_adj = upstream + after_inner
    branch_adj = (scale_one * after_adj).astype(bf16)

    attended_adj = against(branch_adj, out_w).astype(bf16)
    attended_adj = trade(attended_adj.reshape(rows, group, part).transpose(1, 0, 2), SHARD)
    mixed_adj = attend_backward(mixed, lse, attended_adj.reshape(length, part), scaling)
    in_weight_adj = across(hidden, mixed_adj)
    hidden_part = against(mixed_adj, in_w)
    hidden_sent = trade(hidden_part.astype(bf16).reshape(group, rows, width), SHARD)

    piece = part // 8

    def chip_rows(array):
        return core_sum(array.reshape(group, 2, NX, piece, array.shape[-1]))

    def x_sum(array):
        return return_x([pick(array, (x + k) % NX, 1) for k in range(NX)]).astype(bf16)

    out_sum = x_sum(chip_rows(across(attended, branch_adj).astype(bf16)))

    sums = jnp.sum(mixed_adj.astype(f32), axis=0)
    pairs = jnp.zeros((width,), f32)
    pairs = lax.dynamic_update_slice(pairs, sums[:part], ((me // 2) * part,))
    pairs = lax.dynamic_update_slice(pairs, sums[2 * part :], (width // 2 + (me // 2) * part,))
    even = (me % 2 == 0).astype(f32)
    up_sums = jnp.sum(pre_adj.astype(f32), axis=0)
    vectors = [
        jnp.sum(branch_adj.astype(f32), axis=0),
        jnp.sum((scale_two * upstream).astype(bf16).astype(f32), axis=0),
        jnp.sum(hidden_part * normal_one, axis=0),
        jnp.sum(hidden_part, axis=0),
        gain_two_adj,
        shift_two_adj,
        jnp.sum(after_adj * branch, axis=0),
        jnp.sum(upstreams * down_part, axis=0) + jnp.sum(upstream, axis=0) * down_bias,
        pairs * even,
        pairs * (1 - even),
        *[up_sums * (x == j).astype(f32) for j in range(NX)],
    ]
    columns = jnp.stack(vectors).astype(bf16).T
    columns = jnp.pad(columns, ((0, 0), (0, part - columns.shape[1])))
    yl = lax.axis_index("yl")
    last = chip_rows(jnp.concatenate([in_weight_adj.astype(bf16), columns], axis=1))
    pair = total(jnp.stack(after_that(arrived, last))).astype(bf16)
    down = down_part.astype(bf16).reshape(NX, rows, width)
    down = return_x(after_that(down, last)) + down_bias
    layer_output = (after + scale_two * down).astype(bf16)
    pair = add(pick(pair, yl), pick(pair, 1 - yl), "yl")
    last = jnp.concatenate([x_sum(last), out_sum], axis=2)
    hidden_adj = total(after_that(hidden_sent, last))
    _, first_pull = jax.vjp(lambda v: normalised(v) * gain_one, local)
    tokens_adjoint = (after_adj + first_pull(hidden_adj)[0]).astype(bf16)
    pair = add(pair, pair, "yh")
    last = trade(after_that(add(last, last, "yh"), hidden_sent), SHARD)
    matrix = last[:, :, : 3 * part].reshape(group, piece, 3, part).transpose(1, 2, 0, 3).reshape(piece, 3 * width)
    sums = total(last[:, :, 3 * part :]).astype(bf16)
    last = arrivals(jnp.concatenate([matrix, sums], axis=1))
    reduce_weight_adj, expand_weight_adj = finish_pair(arrivals(pair), x, core, part, width)
    input_weight_adj, output_weight_adj, vectors = finish(last, x, core, part, width)

    return (
        layer_output[None],
        tokens_adjoint[None],
        input_weight_adj,
        vectors[8:10].reshape(2 * part),
        output_weight_adj,
        vectors[0],
        expand_weight_adj,
        vectors[10:14].reshape(units),
        reduce_weight_adj,
        vectors[1],
        *[vectors[j] for j in range(2, 8)],
    )


def solution(mesh):
    fine = Mesh(mesh.devices.reshape(2, NX, 2, NZ, 2), REP + SHARD)
    rows = P(REP, SHARD, None)
    matrix, vector = P(SHARD, None), P(SHARD)
    placed = (
        rows,
        matrix,
        vector,
        matrix,
        vector,
        matrix,
        vector,
        matrix,
        *[vector] * 7,
        rows,
    )
    return jax.shard_map(
        shards,
        mesh=fine,
        in_specs=placed,
        out_specs=(
            rows,
            rows,
            matrix,
            vector,
            matrix,
            vector,
            matrix,
            vector,
            matrix,
            *[vector] * 7,
        ),
        check_vma=False,
    )
```

profile of v0, /device:TPU:1, one launch (start us, length us, event | category | flops | bytes accessed | tf_op | source)
XLA Modules:
  0.0 322.6 jit_solution(16137370950451668691)
XLA Ops:
  4.1 2.2 collective-permute-start
  7.9 2.0 pad_maximum_fusion
  9.9 4.9 %collective-permute-done = bf16[192,1024]{1,0:T(8,128)(2,1)} collective-permute-done((bf16[192,1024]{1,0:T(8,128)(2,1)S(1)}, bf16[192,1024]{1,0:T(8,128)(2,1)}, u32[]{:S(2)}, u32[]{:S(2)}) %collective-permute-start) | collective-permute-done | bytes 393248 | tf_op jit(solution)/shard_map/ppermute | solution.py:50
  14.8 6.3 %all-to-all-start = ((bf16[8,184,1024]{2,1,0:T(8,128)(2,1)}), bf16[8,184,1024]{2,1,0:T(8,128)(2,1)}, u32[]{:S(2)}, u32[]{:S(2)}) async-start(bf16[8,184,1024]{2,1,0:T(8,128)(2,1)} %pad_maximum_fusion), calls=%async_computation | async-start | bytes 6029312 | tf_op jit(solution)/shard_map/all_to_all | solution.py:54
  22.4 1.5 collective-permute-start.3
  23.9 2.4 collective-permute-start.2
  27.6 28.8 %all-to-all-done = bf16[8,184,1024]{2,1,0:T(8,128)(2,1)} async-done(((bf16[8,184,1024]{2,1,0:T(8,128)(2,1)}), bf16[8,184,1024]{2,1,0:T(8,128)(2,1)}, u32[]{:S(2)}, u32[]{:S(2)}) %all-to-all-start) | async-done | bytes 3014688 | tf_op jit(solution)/shard_map/all_to_all | solution.py:54
  57.5 1.9 convert_reduce_fusion.1
  59.4 2.3 multiply_reduce_fusion.1
  63.9 2.7 add_convert_fusion.1
  67.9 6.7 %shard_map.279 = (bf16[1024,128]{1,0:T(8,128)(2,1)S(1)}, f32[8,1024]{1,0:T(8,128)S(1)}) custom-call(bf16[1024,384]{1,0:T(8,128)(2,1)S(1)} %add_convert_fusion.3.mixed_ref), custom_call_target="tpu_custom_call" | custom-call | flops 2147483648 | bytes 1048576 | tf_op jit(solution)/shard_map/pallas_call | solution.py:260
  74.7 14.5 %collective-permute-done.2.refs_2_ = bf16[2,192,1024]{2,1,0:T(8,128)(2,1)S(1)} collective-permute-done((bf16[2,192,1024]{2,1,0:T(8,128)(2,1)S(1)}, bf16[2,192,1024]{2,1,0:T(8,128)(2,1)S(1)}, u32[]{:S(2)}, u32[]{:S(2)}) %collective-permute-start.2) | collective-permute-done | bytes 786464 | tf_op jit(solution)/shard_map/ppermute | solution.py:72
  89.2 2.7 collective-permute-start.4
  95.5 4.3 %all-to-all-start.1 = ((bf16[8,128,128]{1,2,0:T(8,128)(2,1)}), bf16[8,128,128]{1,2,0:T(8,128)(2,1)}, u32[]{:S(2)}, u32[]{:S(2)}) async-start(bf16[8,128,128]{1,2,0:T(8,128)(2,1)} %copy.48), calls=%async_computation.1 | async-start | bytes 524288 | tf_op jit(solution)/shard_map/all_to_all | solution.py:54
  99.8 2.5 collective-permute-start.12
  104.7 2.5 shard_map.280
  109.8 2.4 fusion.57
  112.7 2.3 collective-permute-start.9
  115.4 5.4 %collective-permute-done.10 = bf16[128,1024]{1,0:T(8,128)(2,1)S(1)} collective-permute-done((bf16[128,1024]{1,0:T(8,128)(2,1)S(1)}, bf16[128,1024]{1,0:T(8,128)(2,1)S(1)}, u32[]{:S(2)}, u32[]{:S(2)}) %collective-permute-start.10) | collective-permute-done | bytes 262176 | tf_op jit(solution)/shard_map/ppermute | solution.py:72
  121.2 4.6 %collective-permute-done.9 = bf16[128,1024]{1,0:T(8,128)(2,1)S(1)} collective-permute-done((bf16[128,1024]{1,0:T(8,128)(2,1)S(1)}, bf16[128,1024]{1,0:T(8,128)(2,1)S(1)}, u32[]{:S(2)}, u32[]{:S(2)}) %collective-permute-start.9) | collective-permute-done | bytes 262176 | tf_op jit(solution)/shard_map/ppermute | solution.py:72
  126.7 5.5 %multiply_convert_fusion = (bf16[512,1024]{1,0:T(8,128)(2,1)S(1)}, f32[512,1024]{1,0:T(8,128)S(1)}, f32[512,1024]{1,0:T(8,128)S(1)}) fusion(f32[1024]{0:T(1024)S(1)} %fusion.45, bf16[1024,1024]{1,0:T(8,128)(2,1)S(1)} %copy-done.9, bf16[128,1024]{1,0:T(8,128)(2,1)S(1)} %collective-permute-done.10, bf16[128,1024]{1,0:T(8,128)(2,1)S(1)} %collective-permute-done.9, ...), kind=kOutput, calls=%fused_computation.25 | convolution fusion | flops 1112539136 | bytes 8392704 | tf_op jit(solution)/shard_map/dot_general | solution.py:35
  132.2 3.1 convert_reduce_fusion.2
  138.1 4.3 %collective-permute-start.18 = (bf16[8,64,1024]{2,1,0:T(8,128)(2,1)S(1)}, bf16[8,64,1024]{2,1,0:T(8,128)(2,1)S(1)}, u32[]{:S(2)}, u32[]{:S(2)}) collective-permute-start(bf16[8,64,1024]{2,1,0:T(8,128)(2,1)S(1)} %dynamic-slice_bitcast_fusion), channel_id=1, source_target_pairs={{0,8},{8,0},{1,9},{9,1},{2,10},{10,2},{3,11},{11,3},{4,12},{12,4},... | collective-permute-start | bytes 3145736 | tf_op jit(solution)/shard_map/ppermute | solution.py:50
  142.4 2.4 convolution_convert_fusion.1
  145.1 2.8 collective-permute-start.16
  148.0 3.3 %fusion.2 = (f32[1024]{0:T(1024)S(1)}, bf16[512,1024]{1,0:T(8,128)(2,1)}) fusion(bf16[128,1024]{1,0:T(8,128)(2,1)} %collective-permute-done.13, bf16[128,1024]{1,0:T(8,128)(2,1)} %collective-permute-done.12, bf16[128,1024]{1,0:T(8,128)(2,1)S(1)} %collective-permute-done.11, bf16[128,1024]{1,0:T(8,128)(2,1)} %bitcast.32, ...), kind=kOutput, calls=%fused_computation.13 | convolution fusion | flops 1079507968 | bytes 5246976 | tf_op jit(solution)/shard_map/dot_general | solution.py:35
  151.3 3.4 %collective-permute-done.14 = bf16[128,1024]{1,0:T(8,128)(2,1)S(1)} collective-permute-done((bf16[128,1024]{1,0:T(8,128)(2,1)S(1)}, bf16[128,1024]{1,0:T(8,128)(2,1)S(1)}, u32[]{:S(2)}, u32[]{:S(2)}) %collective-permute-start.14) | collective-permute-done | bytes 262176 | tf_op jit(solution)/shard_map/ppermute | solution.py:76
  154.7 3.7 %collective-permute-done.15 = bf16[128,1024]{1,0:T(8,128)(2,1)S(1)} collective-permute-done((bf16[128,1024]{1,0:T(8,128)(2,1)S(1)}, bf16[128,1024]{1,0:T(8,128)(2,1)S(1)}, u32[]{:S(2)}, u32[]{:S(2)}) %collective-permute-start.15) | collective-permute-done | bytes 262176 | tf_op jit(solution)/shard_map/ppermute | solution.py:76
  159.4 1.5 pad_maximum_fusion.1
  165.0 6.4 %all-to-all-start.2 = ((bf16[8,128,128]{2,1,0:T(8,128)(2,1)}), bf16[8,128,128]{2,1,0:T(8,128)(2,1)S(1)}, u32[]{:S(2)}, u32[]{:S(2)}) async-start(bf16[8,128,128]{2,1,0:T(8,128)(2,1)} %bitcast.240), calls=%async_computation.2 | async-start | bytes 524288 | tf_op jit(solution)/shard_map/all_to_all | solution.py:54
  171.4 1.5 convert_reduce_fusion.4
  172.9 3.2 copy.55
  176.2 1.4 all-to-all-done.2
  177.6 7.6 %shard_map.281 = bf16[1024,384]{1,0:T(8,128)(2,1)S(1)} custom-call(bf16[1024,384]{1,0:T(8,128)(2,1)S(1)} %copy-done.11, f32[8,1024]{1,0:T(8,128)S(1)} %get-tuple-element.50.lse_ref, bf16[1024,128]{1,0:T(8,128)(2,1)S(1)} %bitcast.244), custom_call_target="tpu_custom_call" | custom-call | flops 5368709120 | bytes 2097152 | tf_op jit(solution)/shard_map/pallas_call | solution.py:276
  185.8 4.3 %fusion.53 = (bf16[1024]{0:T(1024)(128)(2,1)S(1)}, bf16[1024]{0:T(1024)(128)(2,1)S(1)}, bf16[1024,1024]{1,0:T(8,128)(2,1)}, bf16[1024,1024]{1,0:T(8,128)(2,1)S(1)}) fusion(f32[1024]{0:T(1024)S(1)} %get-tuple-element.134, f32[1024]{0:T(1024)S(1)} %get-tuple-element.132, bf16[8,184,1024]{2,1,0:T(8,128)(2,1)} %all-to-all-done, ...), kind=kOutput, calls=%fused_computation.192 | convolution fusion | flops 815790080 | bytes 7884800 | tf_op jit(solution)/shard_map/dot_general | solution.py:39
  192.9 2.7 collective-permute-start.19
  195.7 1.6 convolution_convert_fusion.2
  203.6 4.8 %all-to-all-start.3 = ((bf16[8,128,1024]{2,1,0:T(8,128)(2,1)}), bf16[8,128,1024]{2,1,0:T(8,128)(2,1)S(1)}, u32[]{:S(2)}, u32[]{:S(2)}) async-start(bf16[8,128,1024]{2,1,0:T(8,128)(2,1)} %bitcast.257), calls=%async_computation.3 | async-start | bytes 4194304 | tf_op jit(solution)/shard_map/all_to_all | solution.py:54
  208.5 1.5 fusion.17
  211.0 4.8 %collective-permute-done.40 = bf16[2,128,1024]{2,1,0:T(8,128)(2,1)} collective-permute-done((bf16[2,128,1024]{2,1,0:T(8,128)(2,1)}, bf16[2,128,1024]{2,1,0:T(8,128)(2,1)}, u32[]{:S(2)}, u32[]{:S(2)}) %collective-permute-start.40) | collective-permute-done | bytes 524320 | tf_op jit(solution)/shard_map/ppermute | solution.py:76
  215.8 2.9 collective-permute-start.25
  218.6 21.9 %collective-permute-done.38 = bf16[2,128,1024]{2,1,0:T(8,128)(2,1)} collective-permute-done((bf16[2,128,1024]{2,1,0:T(8,128)(2,1)}, bf16[2,128,1024]{2,1,0:T(8,128)(2,1)}, u32[]{:S(2)}, u32[]{:S(2)}) %collective-permute-start.38) | collective-permute-done | bytes 524320 | tf_op jit(solution)/shard_map/ppermute | solution.py:76
  241.4 1.5 add_add_fusion.2
  244.1 1.5 fusion.4
  245.8 2.7 collective-permute-start.29
  248.4 2.1 collective-permute-start.28
  250.6 1.7 collective-permute-start.22
  252.4 2.6 collective-permute-done.27
  255.7 2.6 collective-permute-start.42
  258.3 3.4 %collective-permute-done.28 = bf16[8,16,1024]{2,1,0:T(8,128)(2,1)S(1)} collective-permute-done((bf16[8,16,1024]{2,1,0:T(8,128)(2,1)S(1)}, bf16[8,16,1024]{2,1,0:T(8,128)(2,1)S(1)}, u32[]{:S(2)}, u32[]{:S(2)}) %collective-permute-start.28) | collective-permute-done | bytes 262176 | tf_op jit(solution)/shard_map/ppermute | solution.py:76
  261.9 2.7 collective-permute-start.30
  264.8 1.4 collective-permute-start.44
  268.5 10.3 %collective-permute-start.46 = (bf16[128,1024]{1,0:T(8,128)(2,1)S(1)}, bf16[128,1024]{1,0:T(8,128)(2,1)S(1)}, u32[]{:S(2)}, u32[]{:S(2)}) collective-permute-start(bf16[128,1024]{1,0:T(8,128)(2,1)S(1)} %add_convert_fusion.5.refs_0_), channel_id=1, source_target_pairs={{0,8},{8,0},{1,9},{9,1},{2,10},{10,2},{3,11},{11,3},{4,12},{12,4},... | collective-permute-start | bytes 786440 | tf_op jit(solution)/shard_map/ppermute | solution.py:50
  278.7 6.4 %collective-permute-start.49 = (bf16[128,1024]{1,0:T(8,128)(2,1)S(1)}, bf16[128,1024]{1,0:T(8,128)(2,1)S(1)}, u32[]{:S(2)}, u32[]{:S(2)}) collective-permute-start(bf16[128,1024]{1,0:T(8,128)(2,1)S(1)} %collective-permute-done.45.refs_3_), channel_id=1, source_target_pairs={{0,8},{8,0},{1,9},{9,1},{2,10},{10,2},{3,11},{11,3},{4,12},{12,4},... | collective-permute-start | bytes 786440 | tf_op jit(solution)/shard_map/ppermute | solution.py:50
  287.0 3.0 shard_map.283
  291.4 4.1 %all-to-all-start.4 = ((bf16[8,16,1536]{2,1,0:T(8,128)(2,1)}), bf16[8,16,1536]{2,1,0:T(8,128)(2,1)}, u32[]{:S(2)}, u32[]{:S(2)}) async-start(bf16[8,16,1536]{2,1,0:T(8,128)(2,1)} %add_convert_fusion.4), calls=%async_computation.4 | async-start | bytes 786432 | tf_op jit(solution)/shard_map/all_to_all | solution.py:54
  295.5 2.0 convert_reduce_fusion
  298.1 5.6 %all-to-all-done.4 = bf16[8,16,1536]{2,1,0:T(8,128)(2,1)} async-done(((bf16[8,16,1536]{2,1,0:T(8,128)(2,1)}), bf16[8,16,1536]{2,1,0:T(8,128)(2,1)}, u32[]{:S(2)}, u32[]{:S(2)}) %all-to-all-start.4) | async-done | bytes 393248 | tf_op jit(solution)/shard_map/all_to_all | solution.py:54
  306.0 3.2 collective-permute-start.32
  309.2 2.0 collective-permute-start.34
  311.2 3.9 %collective-permute-start.37 = (bf16[16,4224]{1,0:T(8,128)(2,1)S(1)}, bf16[16,4224]{1,0:T(8,128)(2,1)S(1)}, u32[]{:S(2)}, u32[]{:S(2)}) collective-permute-start(bf16[16,4224]{1,0:T(8,128)(2,1)S(1)} %collective-permute-done.33.refs_3_), channel_id=1, source_target_pairs={{0,8},{8,0},{1,9},{9,1},{2,10},{10,2},{3,11},{11,3},{4,12},{12,4},... | collective-permute-start | bytes 405512 | tf_op jit(solution)/shard_map/ppermute | solution.py:50
  315.1 1.6 collective-permute-start.36
  316.6 1.9 fusion.40
  318.6 2.0 shard_map.282
  (251 shorter events, 54.5 us)
Async XLA Ops:
  4.1 10.7 %collective-permute-start = (bf16[192,1024]{1,0:T(8,128)(2,1)S(1)}, bf16[192,1024]{1,0:T(8,128)(2,1)}, u32[]{:S(2)}, u32[]{:S(2)}) collective-permute-start(bf16[192,1024]{1,0:T(8,128)(2,1)S(1)} %pad_maximum_fusion.5), channel_id=1, source_target_pairs={{0,1},{1,0},{2,3},{3,2},{4,5},{5,4},{6,7},{7,6},{8,9},{9,8},{10,11... | collective-permute-start | bytes 1179656 | tf_op jit(solution)/shard_map/ppermute | solution.py:50
  14.8 41.7 %all-to-all-start = ((bf16[8,184,1024]{2,1,0:T(8,128)(2,1)}), bf16[8,184,1024]{2,1,0:T(8,128)(2,1)}, u32[]{:S(2)}, u32[]{:S(2)}) async-start(bf16[8,184,1024]{2,1,0:T(8,128)(2,1)} %pad_maximum_fusion), calls=%async_computation | async-start | bytes 6029312 | tf_op jit(solution)/shard_map/all_to_all | solution.py:54
  22.4 52.3 %collective-permute-start.3 = (bf16[2,192,1024]{2,1,0:T(8,128)(2,1)S(1)}, bf16[2,192,1024]{2,1,0:T(8,128)(2,1)S(1)}, u32[]{:S(2)}, u32[]{:S(2)}) collective-permute-start(bf16[2,192,1024]{2,1,0:T(8,128)(2,1)S(1)} %pad_maximum_fusion.4.refs_0_), channel_id=1, source_target_pairs={{6,0},{0,2},{2,4},{4,6},{7,1},{1,3},{3,5},{5,7},{14,8},{8,10},{10,... | collective-permute-start | bytes 2359304 | tf_op jit(solution)/shard_map/ppermute | solution.py:72
  23.9 65.3 %collective-permute-start.2 = (bf16[2,192,1024]{2,1,0:T(8,128)(2,1)S(1)}, bf16[2,192,1024]{2,1,0:T(8,128)(2,1)S(1)}, u32[]{:S(2)}, u32[]{:S(2)}) collective-permute-start(bf16[2,192,1024]{2,1,0:T(8,128)(2,1)S(1)} %pad_maximum_fusion.4.refs_0_), channel_id=1, source_target_pairs={{4,0},{6,2},{0,4},{2,6},{5,1},{7,3},{1,5},{3,7},{12,8},{14,10},{8,... | collective-permute-start | bytes 2359304 | tf_op jit(solution)/shard_map/ppermute | solution.py:72
  26.3 62.9 %collective-permute-start.1 = (bf16[2,192,1024]{2,1,0:T(8,128)(2,1)S(1)}, bf16[2,192,1024]{2,1,0:T(8,128)(2,1)}, u32[]{:S(2)}, u32[]{:S(2)}) collective-permute-start(bf16[2,192,1024]{2,1,0:T(8,128)(2,1)S(1)} %pad_maximum_fusion.4.refs_0_), channel_id=1, source_target_pairs={{2,0},{4,2},{6,4},{0,6},{3,1},{5,3},{7,5},{1,7},{10,8},{12,10},{14... | collective-permute-start | bytes 2359304 | tf_op jit(solution)/shard_map/ppermute | solution.py:72
  67.9 6.7 %copy-start.10 = (bf16[1024,384]{1,0:T(8,128)(2,1)}, bf16[1024,384]{1,0:T(8,128)(2,1)S(1)}, u32[]{:S(2)}) copy-start(bf16[1024,384]{1,0:T(8,128)(2,1)S(1)} %add_convert_fusion.3.mixed_ref) | copy-start | bytes 2359300
  74.7 27.7 %copy-start.2 = (bf16[2,192,1024]{2,1,0:T(8,128)(2,1)}, bf16[2,192,1024]{2,1,0:T(8,128)(2,1)S(1)}, u32[]{:S(2)}) copy-start(bf16[2,192,1024]{2,1,0:T(8,128)(2,1)S(1)} %collective-permute-done.3.refs_3_) | copy-start | bytes 2359300
  89.2 10.7 %collective-permute-start.4 = (bf16[2,192,1024]{2,1,0:T(8,128)(2,1)S(1)}, bf16[2,192,1024]{2,1,0:T(8,128)(2,1)}, u32[]{:S(2)}, u32[]{:S(2)}) collective-permute-start(bf16[2,192,1024]{2,1,0:T(8,128)(2,1)S(1)} %pad_maximum_fusion.4.refs_0_), channel_id=1, source_target_pairs={{0,8},{8,0},{1,9},{9,1},{2,10},{10,2},{3,11},{11,3},{4,12},{12,4},... | collective-permute-start | bytes 2359304 | tf_op jit(solution)/shard_map/ppermute | solution.py:50
  91.9 10.4 %collective-permute-start.5 = (bf16[2,192,1024]{2,1,0:T(8,128)(2,1)}, bf16[2,192,1024]{2,1,0:T(8,128)(2,1)}, u32[]{:S(2)}, u32[]{:S(2)}) collective-permute-start(bf16[2,192,1024]{2,1,0:T(8,128)(2,1)} %collective-permute-done.1.refs_1_), channel_id=1, source_target_pairs={{0,8},{8,0},{1,9},{9,1},{2,10},{10,2},{3,11},{11,3},{4,12},{12,4},... | collective-permute-start | bytes 2359304 | tf_op jit(solution)/shard_map/ppermute | solution.py:50
  91.9 10.4 %collective-permute-start.6 = (bf16[2,192,1024]{2,1,0:T(8,128)(2,1)S(1)}, bf16[2,192,1024]{2,1,0:T(8,128)(2,1)}, u32[]{:S(2)}, u32[]{:S(2)}) collective-permute-start(bf16[2,192,1024]{2,1,0:T(8,128)(2,1)S(1)} %collective-permute-done.2.refs_2_), channel_id=1, source_target_pairs={{0,8},{8,0},{1,9},{9,1},{2,10},{10,2},{3,11},{11,3},{4,12},{12,4},... | collective-permute-start | bytes 2359304 | tf_op jit(solution)/shard_map/ppermute | solution.py:50
  93.3 9.1 %collective-permute-start.7 = (bf16[2,192,1024]{2,1,0:T(8,128)(2,1)S(1)}, bf16[2,192,1024]{2,1,0:T(8,128)(2,1)}, u32[]{:S(2)}, u32[]{:S(2)}) collective-permute-start(bf16[2,192,1024]{2,1,0:T(8,128)(2,1)S(1)} %collective-permute-done.3.refs_3_), channel_id=1, source_target_pairs={{0,8},{8,0},{1,9},{9,1},{2,10},{10,2},{3,11},{11,3},{4,12},{12,4},... | collective-permute-start | bytes 2359304 | tf_op jit(solution)/shard_map/ppermute | solution.py:50
  93.3 38.9 %collective-permute-start.13 = (bf16[128,1024]{1,0:T(8,128)(2,1)}, bf16[128,1024]{1,0:T(8,128)(2,1)}, u32[]{:S(2)}, u32[]{:S(2)}) collective-permute-start(bf16[128,1024]{1,0:T(8,128)(2,1)} %bitcast.32), channel_id=1, source_target_pairs={{48,0},{0,16},{16,32},{32,48},{49,1},{1,17},{17,33},{33,49},{50,2}... | collective-permute-start | bytes 786440 | tf_op jit(solution)/shard_map/ppermute | solution.py:72
  95.5 14.3 %all-to-all-start.1 = ((bf16[8,128,128]{1,2,0:T(8,128)(2,1)}), bf16[8,128,128]{1,2,0:T(8,128)(2,1)}, u32[]{:S(2)}, u32[]{:S(2)}) async-start(bf16[8,128,128]{1,2,0:T(8,128)(2,1)} %copy.48), calls=%async_computation.1 | async-start | bytes 524288 | tf_op jit(solution)/shard_map/all_to_all | solution.py:54
  99.8 32.4 %collective-permute-start.12 = (bf16[128,1024]{1,0:T(8,128)(2,1)}, bf16[128,1024]{1,0:T(8,128)(2,1)}, u32[]{:S(2)}, u32[]{:S(2)}) collective-permute-start(bf16[128,1024]{1,0:T(8,128)(2,1)} %bitcast.32), channel_id=1, source_target_pairs={{32,0},{48,16},{0,32},{16,48},{33,1},{49,17},{1,33},{17,49},{34,2}... | collective-permute-start | bytes 786440 | tf_op jit(solution)/shard_map/ppermute | solution.py:72
  109.8 16.8 %copy-start.9 = (bf16[1024,1024]{1,0:T(8,128)(2,1)S(1)}, bf16[1024,1024]{1,0:T(8,128)(2,1)}, u32[]{:S(2)}) copy-start(bf16[1024,1024]{1,0:T(8,128)(2,1)} %copy-done.8) | copy-start | bytes 6291460
  112.6 8.2 %collective-permute-start.10 = (bf16[128,1024]{1,0:T(8,128)(2,1)S(1)}, bf16[128,1024]{1,0:T(8,128)(2,1)S(1)}, u32[]{:S(2)}, u32[]{:S(2)}) collective-permute-start(bf16[128,1024]{1,0:T(8,128)(2,1)S(1)} %add_convert_fusion.7), channel_id=1, source_target_pairs={{48,0},{0,16},{16,32},{32,48},{49,1},{1,17},{17,33},{33,49},{50,2}... | collective-permute-start | bytes 786440 | tf_op jit(solution)/shard_map/ppermute | solution.py:72
  112.7 13.1 %collective-permute-start.9 = (bf16[128,1024]{1,0:T(8,128)(2,1)S(1)}, bf16[128,1024]{1,0:T(8,128)(2,1)S(1)}, u32[]{:S(2)}, u32[]{:S(2)}) collective-permute-start(bf16[128,1024]{1,0:T(8,128)(2,1)S(1)} %add_convert_fusion.7), channel_id=1, source_target_pairs={{32,0},{48,16},{0,32},{16,48},{33,1},{49,17},{1,33},{17,49},{34,2}... | collective-permute-start | bytes 786440 | tf_op jit(solution)/shard_map/ppermute | solution.py:72
  115.0 11.6 %collective-permute-start.8 = (bf16[128,1024]{1,0:T(8,128)(2,1)S(1)}, bf16[128,1024]{1,0:T(8,128)(2,1)S(1)}, u32[]{:S(2)}, u32[]{:S(2)}) collective-permute-start(bf16[128,1024]{1,0:T(8,128)(2,1)S(1)} %add_convert_fusion.7), channel_id=1, source_target_pairs={{16,0},{32,16},{48,32},{0,48},{17,1},{33,17},{49,33},{1,49},{18,2}... | collective-permute-start | bytes 786440 | tf_op jit(solution)/shard_map/ppermute | solution.py:72
  120.8 11.5 %collective-permute-start.11 = (bf16[128,1024]{1,0:T(8,128)(2,1)}, bf16[128,1024]{1,0:T(8,128)(2,1)S(1)}, u32[]{:S(2)}, u32[]{:S(2)}) collective-permute-start(bf16[128,1024]{1,0:T(8,128)(2,1)} %bitcast.32), channel_id=1, source_target_pairs={{16,0},{32,16},{48,32},{0,48},{17,1},{33,17},{49,33},{1,49},{18,2}... | collective-permute-start | bytes 786440 | tf_op jit(solution)/shard_map/ppermute | solution.py:72
  138.1 20.5 %collective-permute-start.18 = (bf16[8,64,1024]{2,1,0:T(8,128)(2,1)S(1)}, bf16[8,64,1024]{2,1,0:T(8,128)(2,1)S(1)}, u32[]{:S(2)}, u32[]{:S(2)}) collective-permute-start(bf16[8,64,1024]{2,1,0:T(8,128)(2,1)S(1)} %dynamic-slice_bitcast_fusion), channel_id=1, source_target_pairs={{0,8},{8,0},{1,9},{9,1},{2,10},{10,2},{3,11},{11,3},{4,12},{12,4},... | collective-permute-start | bytes 3145736 | tf_op jit(solution)/shard_map/ppermute | solution.py:50
  144.9 14.1 %collective-permute-start.17 = (bf16[8,64,1024]{2,1,0:T(8,128)(2,1)S(1)}, bf16[8,64,1024]{2,1,0:T(8,128)(2,1)S(1)}, u32[]{:S(2)}, u32[]{:S(2)}) collective-permute-start(bf16[8,64,1024]{2,1,0:T(8,128)(2,1)S(1)} %dynamic-slice_bitcast_fusion.1), channel_id=1, source_target_pairs={{0,8},{8,0},{1,9},{9,1},{2,10},{10,2},{3,11},{11,3},{4,12},{12,4},... | collective-permute-start | bytes 3145736 | tf_op jit(solution)/shard_map/ppermute | solution.py:50
  145.1 9.6 %collective-permute-start.14 = (bf16[128,1024]{1,0:T(8,128)(2,1)S(1)}, bf16[128,1024]{1,0:T(8,128)(2,1)S(1)}, u32[]{:S(2)}, u32[]{:S(2)}) collective-permute-start(bf16[128,1024]{1,0:T(8,128)(2,1)S(1)} %get-tuple-element.97), channel_id=1, source_target_pairs={{0,16},{16,32},{32,48},{48,0},{1,17},{17,33},{33,49},{49,1},{2,18}... | collective-permute-start | bytes 786440 | tf_op jit(solution)/shard_map/ppermute | solution.py:76
  145.1 9.5 %collective-permute-start.16 = (bf16[128,1024]{1,0:T(8,128)(2,1)S(1)}, bf16[128,1024]{1,0:T(8,128)(2,1)S(1)}, u32[]{:S(2)}, u32[]{:S(2)}) collective-permute-start(bf16[128,1024]{1,0:T(8,128)(2,1)S(1)} %get-tuple-element.98), channel_id=1, source_target_pairs={{0,48},{16,0},{32,16},{48,32},{1,49},{17,1},{33,17},{49,33},{2,50}... | collective-permute-start | bytes 786440 | tf_op jit(solution)/shard_map/ppermute | solution.py:76
  148.0 10.4 %collective-permute-start.15 = (bf16[128,1024]{1,0:T(8,128)(2,1)S(1)}, bf16[128,1024]{1,0:T(8,128)(2,1)S(1)}, u32[]{:S(2)}, u32[]{:S(2)}) collective-permute-start(bf16[128,1024]{1,0:T(8,128)(2,1)S(1)} %get-tuple-element.99), channel_id=1, source_target_pairs={{0,32},{16,48},{32,0},{48,16},{1,33},{17,49},{33,1},{49,17},{2,34}... | collective-permute-start | bytes 786440 | tf_op jit(solution)/shard_map/ppermute | solution.py:76
  165.0 12.5 %all-to-all-start.2 = ((bf16[8,128,128]{2,1,0:T(8,128)(2,1)}), bf16[8,128,128]{2,1,0:T(8,128)(2,1)S(1)}, u32[]{:S(2)}, u32[]{:S(2)}) async-start(bf16[8,128,128]{2,1,0:T(8,128)(2,1)} %bitcast.240), calls=%async_computation.2 | async-start | bytes 524288 | tf_op jit(solution)/shard_map/all_to_all | solution.py:54
  177.6 8.2 %copy-start.23 = (bf16[8,8,16,3,128]{4,3,2,1,0:T(4,128)(2,1)S(1)}, bf16[8,8,16,3,128]{4,3,2,1,0:T(4,128)(2,1)}, u32[]{:S(2)}) copy-start(bf16[8,8,16,3,128]{4,3,2,1,0:T(4,128)(2,1)} %copy-done.22) | copy-start | bytes 2359300
  192.0 6.6 %copy-start.18 = (bf16[1024,512]{1,0:T(8,128)(2,1)}, bf16[1024,512]{1,0:T(8,128)(2,1)S(1)}, u32[]{:S(2)}) copy-start(bf16[1024,512]{1,0:T(8,128)(2,1)S(1)} %copy.51) | copy-start | bytes 3145732
  192.9 15.6 %collective-permute-start.19 = (bf16[8,4,16,512]{3,2,1,0:T(8,128)(2,1)}, bf16[8,4,16,512]{3,2,1,0:T(8,128)(2,1)}, u32[]{:S(2)}, u32[]{:S(2)}) collective-permute-start(bf16[8,4,16,512]{3,2,1,0:T(8,128)(2,1)} %dynamic-slice_bitcast_fusion.6), channel_id=1, source_target_pairs={{0,8},{8,0},{1,9},{9,1},{2,10},{10,2},{3,11},{11,3},{4,12},{12,4},... | collective-permute-start | bytes 1572872 | tf_op jit(solution)/shard_map/ppermute | solution.py:50
  199.6 43.3 %collective-permute-start.26 = (bf16[8,4,16,1024]{3,2,0,1:T(8,128)(2,1)}, bf16[8,4,16,1024]{3,2,0,1:T(8,128)(2,1)}, u32[]{:S(2)}, u32[]{:S(2)}) collective-permute-start(bf16[8,4,16,1024]{3,2,0,1:T(8,128)(2,1)} %bitcast.238), channel_id=1, source_target_pairs={{0,8},{8,0},{1,9},{9,1},{2,10},{10,2},{3,11},{11,3},{4,12},{12,4},... | collective-permute-start | bytes 3145736 | tf_op jit(solution)/shard_map/ppermute | solution.py:50
  201.9 13.9 %collective-permute-start.40 = (bf16[2,128,1024]{2,1,0:T(8,128)(2,1)}, bf16[2,128,1024]{2,1,0:T(8,128)(2,1)}, u32[]{:S(2)}, u32[]{:S(2)}) collective-permute-start(bf16[2,128,1024]{2,1,0:T(8,128)(2,1)} %get-tuple-element.83), channel_id=1, source_target_pairs={{0,6},{2,0},{4,2},{6,4},{1,7},{3,1},{5,3},{7,5},{8,14},{10,8},{12,... | collective-permute-start | bytes 1572872 | tf_op jit(solution)/shard_map/ppermute | solution.py:76
  202.5 16.2 %collective-permute-start.39 = (bf16[2,128,1024]{2,1,0:T(8,128)(2,1)}, bf16[2,128,1024]{2,1,0:T(8,128)(2,1)}, u32[]{:S(2)}, u32[]{:S(2)}) collective-permute-start(bf16[2,128,1024]{2,1,0:T(8,128)(2,1)} %get-tuple-element.84), channel_id=1, source_target_pairs={{0,4},{2,6},{4,0},{6,2},{1,5},{3,7},{5,1},{7,3},{8,12},{10,14},{12... | collective-permute-start | bytes 1572872 | tf_op jit(solution)/shard_map/ppermute | solution.py:76
  203.6 37.0 %collective-permute-start.38 = (bf16[2,128,1024]{2,1,0:T(8,128)(2,1)}, bf16[2,128,1024]{2,1,0:T(8,128)(2,1)}, u32[]{:S(2)}, u32[]{:S(2)}) collective-permute-start(bf16[2,128,1024]{2,1,0:T(8,128)(2,1)} %get-tuple-element.85), channel_id=1, source_target_pairs={{0,2},{2,4},{4,6},{6,0},{1,3},{3,5},{5,7},{7,1},{8,10},{10,12},{12... | collective-permute-start | bytes 1572872 | tf_op jit(solution)/shard_map/ppermute | solution.py:76
  203.6 86.4 %all-to-all-start.3 = ((bf16[8,128,1024]{2,1,0:T(8,128)(2,1)}), bf16[8,128,1024]{2,1,0:T(8,128)(2,1)S(1)}, u32[]{:S(2)}, u32[]{:S(2)}) async-start(bf16[8,128,1024]{2,1,0:T(8,128)(2,1)} %bitcast.257), calls=%async_computation.3 | async-start | bytes 4194304 | tf_op jit(solution)/shard_map/all_to_all | solution.py:54
  208.5 32.9 %copy-start.21 = (bf16[2,128,1024]{2,1,0:T(8,128)(2,1)S(1)}, bf16[2,128,1024]{2,1,0:T(8,128)(2,1)}, u32[]{:S(2)}) copy-start(bf16[2,128,1024]{2,1,0:T(8,128)(2,1)} %get-tuple-element.58) | copy-start | bytes 1572868
  210.1 34.0 %copy-start.17 = (bf16[8,1,4,16,1024]{4,3,2,1,0:T(8,128)(2,1)S(1)}, bf16[8,1,4,16,1024]{4,3,2,1,0:T(8,128)(2,1)}, u32[]{:S(2)}) copy-start(bf16[8,1,4,16,1024]{4,3,2,1,0:T(8,128)(2,1)} %get-tuple-element.87) | copy-start | bytes 3145732
  210.1 35.6 %collective-permute-start.23 = (bf16[8,16,512]{2,1,0:T(8,128)(2,1)S(1)}, bf16[8,16,512]{2,1,0:T(8,128)(2,1)S(1)}, u32[]{:S(2)}, u32[]{:S(2)}) collective-permute-start(bf16[8,16,512]{2,1,0:T(8,128)(2,1)S(1)} %get-tuple-element.102), channel_id=1, source_target_pairs={{0,16},{16,32},{32,48},{48,0},{1,17},{17,33},{33,49},{49,1},{2,18}... | collective-permute-start | bytes 393224 | tf_op jit(solution)/shard_map/ppermute | solution.py:76
  215.8 30.0 %collective-permute-start.25 = (bf16[8,16,512]{2,1,0:T(8,128)(2,1)S(1)}, bf16[8,16,512]{2,1,0:T(8,128)(2,1)S(1)}, u32[]{:S(2)}, u32[]{:S(2)}) collective-permute-start(bf16[8,16,512]{2,1,0:T(8,128)(2,1)S(1)} %get-tuple-element.103), channel_id=1, source_target_pairs={{0,48},{16,0},{32,16},{48,32},{1,49},{17,1},{33,17},{49,33},{2,50}... | collective-permute-start | bytes 393224 | tf_op jit(solution)/shard_map/ppermute | solution.py:76
  218.6 29.8 %collective-permute-start.24 = (bf16[8,16,512]{2,1,0:T(8,128)(2,1)S(1)}, bf16[8,16,512]{2,1,0:T(8,128)(2,1)S(1)}, u32[]{:S(2)}, u32[]{:S(2)}) collective-permute-start(bf16[8,16,512]{2,1,0:T(8,128)(2,1)S(1)} %get-tuple-element.104), channel_id=1, source_target_pairs={{0,32},{16,48},{32,0},{48,16},{1,33},{17,49},{33,1},{49,17},{2,34}... | collective-permute-start | bytes 393224 | tf_op jit(solution)/shard_map/ppermute | solution.py:76
  240.6 24.2 %collective-permute-start.20 = (bf16[128,1024]{1,0:T(8,128)(2,1)S(1)}, bf16[128,1024]{1,0:T(8,128)(2,1)S(1)}, u32[]{:S(2)}, u32[]{:S(2)}) collective-permute-start(bf16[128,1024]{1,0:T(8,128)(2,1)S(1)} %get-tuple-element.94), channel_id=1, source_target_pairs={{0,16},{16,32},{32,48},{48,0},{1,17},{17,33},{33,49},{49,1},{2,18}... | collective-permute-start | bytes 786440 | tf_op jit(solution)/shard_map/ppermute | solution.py:76
  242.9 7.7 %collective-permute-start.41 = (bf16[128,1024]{1,0:T(8,128)(2,1)S(1)}, bf16[128,1024]{1,0:T(8,128)(2,1)S(1)}, u32[]{:S(2)}, u32[]{:S(2)}) collective-permute-start(bf16[128,1024]{1,0:T(8,128)(2,1)S(1)} %dynamic-slice_bitcast_fusion.7), channel_id=1, source_target_pairs={{0,1},{1,0},{2,3},{3,2},{4,5},{5,4},{6,7},{7,6},{8,9},{9,8},{10,11... | collective-permute-start | bytes 786440 | tf_op jit(solution)/shard_map/ppermute | solution.py:50
  245.7 9.3 %collective-permute-start.27 = (bf16[8,16,1024]{2,1,0:T(8,128)(2,1)S(1)}, bf16[8,16,1024]{2,1,0:T(8,128)(2,1)S(1)}, u32[]{:S(2)}, u32[]{:S(2)}) collective-permute-start(bf16[8,16,1024]{2,1,0:T(8,128)(2,1)S(1)} %get-tuple-element.91), channel_id=1, source_target_pairs={{0,16},{16,32},{32,48},{48,0},{1,17},{17,33},{33,49},{49,1},{2,18}... | collective-permute-start | bytes 786440 | tf_op jit(solution)/shard_map/ppermute | solution.py:76
  245.8 9.9 %collective-permute-start.29 = (bf16[8,16,1024]{2,1,0:T(8,128)(2,1)S(1)}, bf16[8,16,1024]{2,1,0:T(8,128)(2,1)S(1)}, u32[]{:S(2)}, u32[]{:S(2)}) collective-permute-start(bf16[8,16,1024]{2,1,0:T(8,128)(2,1)S(1)} %get-tuple-element.92), channel_id=1, source_target_pairs={{0,48},{16,0},{32,16},{48,32},{1,49},{17,1},{33,17},{49,33},{2,50}... | collective-permute-start | bytes 786440 | tf_op jit(solution)/shard_map/ppermute | solution.py:76
  248.4 13.3 %collective-permute-start.28 = (bf16[8,16,1024]{2,1,0:T(8,128)(2,1)S(1)}, bf16[8,16,1024]{2,1,0:T(8,128)(2,1)S(1)}, u32[]{:S(2)}, u32[]{:S(2)}) collective-permute-start(bf16[8,16,1024]{2,1,0:T(8,128)(2,1)S(1)} %get-tuple-element.93), channel_id=1, source_target_pairs={{0,32},{16,48},{32,0},{48,16},{1,33},{17,49},{33,1},{49,17},{2,34}... | collective-permute-start | bytes 786440 | tf_op jit(solution)/shard_map/ppermute | solution.py:76
  250.6 15.6 %collective-permute-start.22 = (bf16[128,1024]{1,0:T(8,128)(2,1)S(1)}, bf16[128,1024]{1,0:T(8,128)(2,1)S(1)}, u32[]{:S(2)}, u32[]{:S(2)}) collective-permute-start(bf16[128,1024]{1,0:T(8,128)(2,1)S(1)} %get-tuple-element.95), channel_id=1, source_target_pairs={{0,48},{16,0},{32,16},{48,32},{1,49},{17,1},{33,17},{49,33},{2,50}... | collective-permute-start | bytes 786440 | tf_op jit(solution)/shard_map/ppermute | solution.py:76
  254.9 12.6 %collective-permute-start.21 = (bf16[128,1024]{1,0:T(8,128)(2,1)S(1)}, bf16[128,1024]{1,0:T(8,128)(2,1)S(1)}, u32[]{:S(2)}, u32[]{:S(2)}) collective-permute-start(bf16[128,1024]{1,0:T(8,128)(2,1)S(1)} %get-tuple-element.96), channel_id=1, source_target_pairs={{0,32},{16,48},{32,0},{48,16},{1,33},{17,49},{33,1},{49,17},{2,34}... | collective-permute-start | bytes 786440 | tf_op jit(solution)/shard_map/ppermute | solution.py:76
  255.7 8.9 %collective-permute-start.42 = (bf16[128,1024]{1,0:T(8,128)(2,1)S(1)}, bf16[128,1024]{1,0:T(8,128)(2,1)S(1)}, u32[]{:S(2)}, u32[]{:S(2)}) collective-permute-start(bf16[128,1024]{1,0:T(8,128)(2,1)S(1)} %fusion.34), channel_id=1, source_target_pairs={{0,64},{64,0},{1,65},{65,1},{2,66},{66,2},{3,67},{67,3},{4,68},{68... | collective-permute-start | bytes 786440 | tf_op jit(solution)/shard_map/ppermute | solution.py:50
  261.9 23.9 %collective-permute-start.30 = (bf16[8,16,1536]{2,1,0:T(8,128)(2,1)S(1)}, bf16[8,16,1536]{2,1,0:T(8,128)(2,1)S(1)}, u32[]{:S(2)}, u32[]{:S(2)}) collective-permute-start(bf16[8,16,1536]{2,1,0:T(8,128)(2,1)S(1)} %pad_maximum_fusion.6), channel_id=1, source_target_pairs={{0,64},{64,0},{1,65},{65,1},{2,66},{66,2},{3,67},{67,3},{4,68},{68... | collective-permute-start | bytes 1179656 | tf_op jit(solution)/shard_map/ppermute | solution.py:50
  264.7 14.1 %collective-permute-start.45 = (bf16[128,1024]{1,0:T(8,128)(2,1)S(1)}, bf16[128,1024]{1,0:T(8,128)(2,1)S(1)}, u32[]{:S(2)}, u32[]{:S(2)}) collective-permute-start(bf16[128,1024]{1,0:T(8,128)(2,1)S(1)} %add_convert_fusion.5.refs_0_), channel_id=1, source_target_pairs={{48,0},{0,16},{16,32},{32,48},{49,1},{1,17},{17,33},{33,49},{50,2}... | collective-permute-start | bytes 786440 | tf_op jit(solution)/shard_map/ppermute | solution.py:72
  264.8 20.4 %collective-permute-start.44 = (bf16[128,1024]{1,0:T(8,128)(2,1)S(1)}, bf16[128,1024]{1,0:T(8,128)(2,1)S(1)}, u32[]{:S(2)}, u32[]{:S(2)}) collective-permute-start(bf16[128,1024]{1,0:T(8,128)(2,1)S(1)} %add_convert_fusion.5.refs_0_), channel_id=1, source_target_pairs={{32,0},{48,16},{0,32},{16,48},{33,1},{49,17},{1,33},{17,49},{34,2}... | collective-permute-start | bytes 786440 | tf_op jit(solution)/shard_map/ppermute | solution.py:72
  266.2 19.0 %collective-permute-start.43 = (bf16[128,1024]{1,0:T(8,128)(2,1)S(1)}, bf16[128,1024]{1,0:T(8,128)(2,1)S(1)}, u32[]{:S(2)}, u32[]{:S(2)}) collective-permute-start(bf16[128,1024]{1,0:T(8,128)(2,1)S(1)} %add_convert_fusion.5.refs_0_), channel_id=1, source_target_pairs={{16,0},{32,16},{48,32},{0,48},{17,1},{33,17},{49,33},{1,49},{18,2}... | collective-permute-start | bytes 786440 | tf_op jit(solution)/shard_map/ppermute | solution.py:72
  268.5 18.2 %collective-permute-start.46 = (bf16[128,1024]{1,0:T(8,128)(2,1)S(1)}, bf16[128,1024]{1,0:T(8,128)(2,1)S(1)}, u32[]{:S(2)}, u32[]{:S(2)}) collective-permute-start(bf16[128,1024]{1,0:T(8,128)(2,1)S(1)} %add_convert_fusion.5.refs_0_), channel_id=1, source_target_pairs={{0,8},{8,0},{1,9},{9,1},{2,10},{10,2},{3,11},{11,3},{4,12},{12,4},... | collective-permute-start | bytes 786440 | tf_op jit(solution)/shard_map/ppermute | solution.py:50
  278.7 7.9 %collective-permute-start.49 = (bf16[128,1024]{1,0:T(8,128)(2,1)S(1)}, bf16[128,1024]{1,0:T(8,128)(2,1)S(1)}, u32[]{:S(2)}, u32[]{:S(2)}) collective-permute-start(bf16[128,1024]{1,0:T(8,128)(2,1)S(1)} %collective-permute-done.45.refs_3_), channel_id=1, source_target_pairs={{0,8},{8,0},{1,9},{9,1},{2,10},{10,2},{3,11},{11,3},{4,12},{12,4},... | collective-permute-start | bytes 786440 | tf_op jit(solution)/shard_map/ppermute | solution.py:50
  285.1 1.5 collective-permute-start.48
  285.2 1.8 collective-permute-start.47
  291.4 12.3 %all-to-all-start.4 = ((bf16[8,16,1536]{2,1,0:T(8,128)(2,1)}), bf16[8,16,1536]{2,1,0:T(8,128)(2,1)}, u32[]{:S(2)}, u32[]{:S(2)}) async-start(bf16[8,16,1536]{2,1,0:T(8,128)(2,1)} %add_convert_fusion.4), calls=%async_computation.4 | async-start | bytes 786432 | tf_op jit(solution)/shard_map/all_to_all | solution.py:54
  297.5 19.1 %copy-start.15 = (f32[128,1024]{1,0:T(8,128)S(1)}, f32[128,1024]{1,0:T(8,128)}, u32[]{:S(2)}) copy-start(f32[128,1024]{1,0:T(8,128)} %copy-done.14) | copy-start | bytes 1572868
  303.7 18.6 %copy-start.1 = (bf16[128,4096]{1,0:T(8,128)(2,1)S(1)}, bf16[128,4096]{1,0:T(8,128)(2,1)}, u32[]{:S(2)}) copy-start(bf16[128,4096]{1,0:T(8,128)(2,1)} %param.21) | copy-start | bytes 3145732
  305.9 5.3 %collective-permute-start.33 = (bf16[16,4224]{1,0:T(8,128)(2,1)S(1)}, bf16[16,4224]{1,0:T(8,128)(2,1)S(1)}, u32[]{:S(2)}, u32[]{:S(2)}) collective-permute-start(bf16[16,4224]{1,0:T(8,128)(2,1)S(1)} %pad_maximum_fusion.10.refs_0_), channel_id=1, source_target_pairs={{48,0},{0,16},{16,32},{32,48},{49,1},{1,17},{17,33},{33,49},{50,2}... | collective-permute-start | bytes 405512 | tf_op jit(solution)/shard_map/ppermute | solution.py:72
  306.0 9.1 %collective-permute-start.32 = (bf16[16,4224]{1,0:T(8,128)(2,1)S(1)}, bf16[16,4224]{1,0:T(8,128)(2,1)S(1)}, u32[]{:S(2)}, u32[]{:S(2)}) collective-permute-start(bf16[16,4224]{1,0:T(8,128)(2,1)S(1)} %pad_maximum_fusion.10.refs_0_), channel_id=1, source_target_pairs={{32,0},{48,16},{0,32},{16,48},{33,1},{49,17},{1,33},{17,49},{34,2}... | collective-permute-start | bytes 405512 | tf_op jit(solution)/shard_map/ppermute | solution.py:72
  309.2 7.4 %collective-permute-start.31 = (bf16[16,4224]{1,0:T(8,128)(2,1)S(1)}, bf16[16,4224]{1,0:T(8,128)(2,1)S(1)}, u32[]{:S(2)}, u32[]{:S(2)}) collective-permute-start(bf16[16,4224]{1,0:T(8,128)(2,1)S(1)} %pad_maximum_fusion.10.refs_0_), channel_id=1, source_target_pairs={{16,0},{32,16},{48,32},{0,48},{17,1},{33,17},{49,33},{1,49},{18,2}... | collective-permute-start | bytes 405512 | tf_op jit(solution)/shard_map/ppermute | solution.py:72
  309.2 9.4 %collective-permute-start.34 = (bf16[16,4224]{1,0:T(8,128)(2,1)S(1)}, bf16[16,4224]{1,0:T(8,128)(2,1)S(1)}, u32[]{:S(2)}, u32[]{:S(2)}) collective-permute-start(bf16[16,4224]{1,0:T(8,128)(2,1)S(1)} %pad_maximum_fusion.10.refs_0_), channel_id=1, source_target_pairs={{0,8},{8,0},{1,9},{9,1},{2,10},{10,2},{3,11},{11,3},{4,12},{12,4},... | collective-permute-start | bytes 405512 | tf_op jit(solution)/shard_map/ppermute | solution.py:50
  311.2 7.4 %collective-permute-start.37 = (bf16[16,4224]{1,0:T(8,128)(2,1)S(1)}, bf16[16,4224]{1,0:T(8,128)(2,1)S(1)}, u32[]{:S(2)}, u32[]{:S(2)}) collective-permute-start(bf16[16,4224]{1,0:T(8,128)(2,1)S(1)} %collective-permute-done.33.refs_3_), channel_id=1, source_target_pairs={{0,8},{8,0},{1,9},{9,1},{2,10},{10,2},{3,11},{11,3},{4,12},{12,4},... | collective-permute-start | bytes 405512 | tf_op jit(solution)/shard_map/ppermute | solution.py:50
  315.1 3.6 %collective-permute-start.36 = (bf16[16,4224]{1,0:T(8,128)(2,1)S(1)}, bf16[16,4224]{1,0:T(8,128)(2,1)S(1)}, u32[]{:S(2)}, u32[]{:S(2)}) collective-permute-start(bf16[16,4224]{1,0:T(8,128)(2,1)S(1)} %collective-permute-done.32.refs_2_), channel_id=1, source_target_pairs={{0,8},{8,0},{1,9},{9,1},{2,10},{10,2},{3,11},{11,3},{4,12},{12,4},... | collective-permute-start | bytes 405512 | tf_op jit(solution)/shard_map/ppermute | solution.py:50
  316.6 2.0 collective-permute-start.35
  (28 other events, 62.1 us)
where the time goes:
time: 328 us; the launch traced here: 323 us
  waiting for transfers between devices  106 us (32%)
  starting transfers between devices  104 us (32%)
  other arithmetic  29.9 us (9%)
  local copies, waits for them, and re-layouts  29.4 us (9%)
  matrix products  28.5 us (9%)
  Pallas kernels  21.8 us (7%)
    ppermute x20, starting transfers between devices, swap(): return lax.ppermute(block, axis, SWAP)  43.8 us
    ppermute x15, waiting for transfers between devices, give(): return lax.ppermute(block, axis, [(i, (i + k) % n) for i in range(n)])  39.8 us
    all_to_all x5, waiting for transfers between devices, trade(): return lax.all_to_all(parts, axes, split_axis=0, concat_axis=0, tiled=True)  35.9 us
    all_to_all x5, starting transfers between devices, trade(): return lax.all_to_all(parts, axes, split_axis=0, concat_axis=0, tiled=True)  25.9 us
    ppermute x15, waiting for transfers between devices, ahead(): return lax.ppermute(block, axis, [((i + k) % n, i) for i in range(n)])  25.4 us
    ppermute x15, starting transfers between devices, ahead(): return lax.ppermute(block, axis, [((i + k) % n, i) for i in range(n)])  18.3 us
    ppermute x15, starting transfers between devices, give(): return lax.ppermute(block, axis, [(i, (i + k) % n) for i in range(n)])  16.4 us
    dot_general x4, matrix products, times(): return jnp.dot(left, right, preferred_element_type=f32)  12.5 us
  transfers between devices with their start and end apart: 55, of which 15 were waited for; matrix products, arithmetic and copies ran while one was open for 16% of the time, Pallas kernels for 4%

commit v1 on v0

--- a/solution.py
+++ b/solution.py
@@ -96,8 +96,10 @@
     return [pick(parts, z)] + [give(pick(parts, (z + k) % NZ), "z", NZ, k) for k in range(1, NZ)]
 
 
-def arrivals(block):
+def arrivals(block, earlier=None):
     blocks = [block] + [ahead(block, "x", NX, k) for k in range(1, NX)]
+    if earlier is not None:
+        blocks = after_that(blocks, earlier)
     return blocks + [swap(b, "core") for b in blocks]
 
 
@@ -409,20 +411,26 @@
 
     attended_adj = against(branch_adj, out_w).astype(bf16)
     attended_adj = trade(attended_adj.reshape(rows, group, part).transpose(1, 0, 2), SHARD)
+    piece = part // 8
+
+    def chip_rows(array):
+        return core_sum(array.reshape(group, 2, NX, piece, array.shape[-1]))
+
+    def x_sum(array):
+        return return_x([pick(array, (x + k) % NX, 1) for k in range(NX)]).astype(bf16)
+
+    out_sum = x_sum(chip_rows(across(attended, branch_adj).astype(bf16)))
+
+    yl = lax.axis_index("yl")
+    pair = total(jnp.stack(arrived)).astype(bf16)
+    attended_adj, pair = lax.optimization_barrier((attended_adj, pair))
     mixed_adj = attend_backward(mixed, lse, attended_adj.reshape(length, part), scaling)
+    pair = add(pick(pair, yl), pick(pair, 1 - yl), "yl")
+    mixed_adj, pair, out_sum = lax.optimization_barrier((mixed_adj, pair, out_sum))
+    pair = add(pair, pair, "yh")
     in_weight_adj = across(hidden, mixed_adj)
     hidden_part = against(mixed_adj, in_w)
     hidden_sent = trade(hidden_part.astype(bf16).reshape(group, rows, width), SHARD)
-
-    piece = part // 8
-
-    def chip_rows(array):
-        return core_sum(array.reshape(group, 2, NX, piece, array.shape[-1]))
-
-    def x_sum(array):
-        return return_x([pick(array, (x + k) % NX, 1) for k in range(NX)]).astype(bf16)
-
-    out_sum = x_sum(chip_rows(across(attended, branch_adj).astype(bf16)))
 
     sums = jnp.sum(mixed_adj.astype(f32), axis=0)
     pairs = jnp.zeros((width,), f32)
@@ -445,23 +453,20 @@
     ]
     columns = jnp.stack(vectors).astype(bf16).T
     columns = jnp.pad(columns, ((0, 0), (0, part - columns.shape[1])))
-    yl = lax.axis_index("yl")
-    last = chip_rows(jnp.concatenate([in_weight_adj.astype(bf16), columns], axis=1))
-    pair = total(jnp.stack(after_that(arrived, last))).astype(bf16)
+    last = chip_rows(after_that(jnp.concatenate([in_weight_adj.astype(bf16), columns], axis=1), pair))
+    last = jnp.concatenate([x_sum(last), out_sum], axis=2)
+    summed = last
     down = down_part.astype(bf16).reshape(NX, rows, width)
-    down = return_x(after_that(down, last)) + down_bias
+    down = return_x(after_that(down, summed)) + down_bias
     layer_output = (after + scale_two * down).astype(bf16)
-    pair = add(pick(pair, yl), pick(pair, 1 - yl), "yl")
-    last = jnp.concatenate([x_sum(last), out_sum], axis=2)
     hidden_adj = total(after_that(hidden_sent, last))
     _, first_pull = jax.vjp(lambda v: normalised(v) * gain_one, local)
     tokens_adjoint = (after_adj + first_pull(hidden_adj)[0]).astype(bf16)
-    pair = add(pair, pair, "yh")
     last = trade(after_that(add(last, last, "yh"), hidden_sent), SHARD)
     matrix = last[:, :, : 3 * part].reshape(group, piece, 3, part).transpose(1, 2, 0, 3).reshape(piece, 3 * width)
     sums = total(last[:, :, 3 * part :]).astype(bf16)
     last = arrivals(jnp.concatenate([matrix, sums], axis=1))
-    reduce_weight_adj, expand_weight_adj = finish_pair(arrivals(pair), x, core, part, width)
+    reduce_weight_adj, expand_weight_adj = finish_pair(arrivals(pair, summed), x, core, part, width)
     input_weight_adj, output_weight_adj, vectors = finish(last, x, core, part, width)
 
     return (

time: 328 us -> 315 us (0.960)
  starting transfers between devices: 104 us -> 96.3 us
  local copies, waits for them, and re-layouts: 29.4 us -> 22.2 us
  waiting for transfers between devices: 106 us -> 111 us
    ppermute x20, starting transfers between devices: 43.8 us -> 32.2 us  [swap(): return lax.ppermute(block, axis, SWAP)]
    ppermute x15, waiting for transfers between devices: 25.4 us -> 35.1 us  [ahead(): return lax.ppermute(block, axis, [((i + k) % n, i) for i in range(n)])]
    ppermute x15, waiting for transfers between devices: 39.8 us -> 32.6 us  [give(): return lax.ppermute(block, axis, [(i, (i + k) % n) for i in range(n)])]
    ppermute x20, waiting for transfers between devices: 5.38 us -> 10.3 us  [swap(): return lax.ppermute(block, axis, SWAP)]
    unnamed x81 -> x71, local copies, waits for them, and re-layouts: 10.5 us -> 7.48 us
  transfers between devices with their start and end apart: 55 -> 55, of which waited for: 15 -> 19; matrix products, arithmetic and copies ran while one was open for 16% -> 15% of each run, Pallas kernels for 4% -> 6%
where the time goes in v1:
time: 315 us; the launch traced here: 310 us
  waiting for transfers between devices  111 us (35%)
  starting transfers between devices  96.3 us (31%)
  other arithmetic  29.1 us (9%)
  matrix products  27.7 us (9%)
  local copies, waits for them, and re-layouts  22.2 us (7%)
  Pallas kernels  21.7 us (7%)
    ppermute x15, waiting for transfers between devices, ahead(): return lax.ppermute(block, axis, [((i + k) % n, i) for i in range(n)])  35.1 us
    all_to_all x5, waiting for transfers between devices, trade(): return lax.all_to_all(parts, axes, split_axis=0, concat_axis=0, tiled=True)  33.1 us
    ppermute x15, waiting for transfers between devices, give(): return lax.ppermute(block, axis, [(i, (i + k) % n) for i in range(n)])  32.6 us
    ppermute x20, starting transfers between devices, swap(): return lax.ppermute(block, axis, SWAP)  32.2 us
    all_to_all x5, starting transfers between devices, trade(): return lax.all_to_all(parts, axes, split_axis=0, concat_axis=0, tiled=True)  23.7 us
    ppermute x15, starting transfers between devices, ahead(): return lax.ppermute(block, axis, [((i + k) % n, i) for i in range(n)])  20.8 us
    ppermute x15, starting transfers between devices, give(): return lax.ppermute(block, axis, [(i, (i + k) % n) for i in range(n)])  19.6 us
    dot_general x4, matrix products, times(): return jnp.dot(left, right, preferred_element_type=f32)  11.8 us
  transfers between devices with their start and end apart: 55, of which 19 were waited for; matrix products, arithmetic and copies ran while one was open for 15% of the time, Pallas kernels for 6%

profile of v1, /device:TPU:1, one launch (start us, length us, event | category | flops | bytes accessed | tf_op | source)
XLA Modules:
  0.0 310.0 jit_solution(17284589610642274209)
XLA Ops:
  4.1 2.2 collective-permute-start
  7.9 2.0 pad_maximum_fusion
  9.9 5.0 %collective-permute-done = bf16[192,1024]{1,0:T(8,128)(2,1)} collective-permute-done((bf16[192,1024]{1,0:T(8,128)(2,1)S(1)}, bf16[192,1024]{1,0:T(8,128)(2,1)}, u32[]{:S(2)}, u32[]{:S(2)}) %collective-permute-start) | collective-permute-done | bytes 393248 | tf_op jit(solution)/shard_map/ppermute | solution.py:50
  14.8 6.3 %all-to-all-start = ((bf16[8,184,1024]{2,1,0:T(8,128)(2,1)}), bf16[8,184,1024]{2,1,0:T(8,128)(2,1)}, u32[]{:S(2)}, u32[]{:S(2)}) async-start(bf16[8,184,1024]{2,1,0:T(8,128)(2,1)} %pad_maximum_fusion), calls=%async_computation | async-start | bytes 6029312 | tf_op jit(solution)/shard_map/all_to_all | solution.py:54
  23.9 2.4 collective-permute-start.2
  27.6 28.8 %all-to-all-done = bf16[8,184,1024]{2,1,0:T(8,128)(2,1)} async-done(((bf16[8,184,1024]{2,1,0:T(8,128)(2,1)}), bf16[8,184,1024]{2,1,0:T(8,128)(2,1)}, u32[]{:S(2)}, u32[]{:S(2)}) %all-to-all-start) | async-done | bytes 3014688 | tf_op jit(solution)/shard_map/all_to_all | solution.py:54
  57.5 1.9 convert_reduce_fusion.1
  59.4 2.3 multiply_reduce_fusion.1
  63.9 2.7 add_convert_fusion.1
  67.9 6.7 %shard_map.279 = (bf16[1024,128]{1,0:T(8,128)(2,1)S(1)}, f32[8,1024]{1,0:T(8,128)S(1)}) custom-call(bf16[1024,384]{1,0:T(8,128)(2,1)S(1)} %add_convert_fusion.3.mixed_ref), custom_call_target="tpu_custom_call" | custom-call | flops 2147483648 | bytes 1048576 | tf_op jit(solution)/shard_map/pallas_call | solution.py:262
  74.6 14.5 %collective-permute-done.2.refs_2_ = bf16[2,192,1024]{2,1,0:T(8,128)(2,1)S(1)} collective-permute-done((bf16[2,192,1024]{2,1,0:T(8,128)(2,1)S(1)}, bf16[2,192,1024]{2,1,0:T(8,128)(2,1)S(1)}, u32[]{:S(2)}, u32[]{:S(2)}) %collective-permute-start.2) | collective-permute-done | bytes 786464 | tf_op jit(solution)/shard_map/ppermute | solution.py:72
  89.2 2.7 collective-permute-start.4
  94.2 4.3 %all-to-all-start.1 = ((bf16[8,128,128]{1,2,0:T(8,128)(2,1)}), bf16[8,128,128]{1,2,0:T(8,128)(2,1)}, u32[]{:S(2)}, u32[]{:S(2)}) async-start(bf16[8,128,128]{1,2,0:T(8,128)(2,1)} %copy.49), calls=%async_computation.1 | async-start | bytes 524288 | tf_op jit(solution)/shard_map/all_to_all | solution.py:54
  99.7 2.5 collective-permute-start.12
  104.5 2.5 shard_map.280
  109.7 1.7 fusion.59
  111.8 2.3 collective-permute-start.9
  114.5 5.4 %collective-permute-done.10 = bf16[128,1024]{1,0:T(8,128)(2,1)S(1)} collective-permute-done((bf16[128,1024]{1,0:T(8,128)(2,1)S(1)}, bf16[128,1024]{1,0:T(8,128)(2,1)S(1)}, u32[]{:S(2)}, u32[]{:S(2)}) %collective-permute-start.10) | collective-permute-done | bytes 262176 | tf_op jit(solution)/shard_map/ppermute | solution.py:72
  120.1 4.8 %collective-permute-done.9 = bf16[128,1024]{1,0:T(8,128)(2,1)S(1)} collective-permute-done((bf16[128,1024]{1,0:T(8,128)(2,1)S(1)}, bf16[128,1024]{1,0:T(8,128)(2,1)S(1)}, u32[]{:S(2)}, u32[]{:S(2)}) %collective-permute-start.9) | collective-permute-done | bytes 262176 | tf_op jit(solution)/shard_map/ppermute | solution.py:72
  125.8 5.5 %multiply_convert_fusion = (bf16[512,1024]{1,0:T(8,128)(2,1)S(1)}, f32[512,1024]{1,0:T(8,128)S(1)}, f32[512,1024]{1,0:T(8,128)S(1)}) fusion(f32[1024]{0:T(1024)S(1)} %fusion.47, bf16[1024,1024]{1,0:T(8,128)(2,1)S(1)} %copy-done.9, bf16[128,1024]{1,0:T(8,128)(2,1)S(1)} %collective-permute-done.10, bf16[128,1024]{1,0:T(8,128)(2,1)S(1)} %collective-permute-done.9, ...), kind=kOutput, calls=%fused_computation.25 | convolution fusion | flops 1112539136 | bytes 8392704 | tf_op jit(solution)/shard_map/dot_general | solution.py:35
  131.3 3.1 convert_reduce_fusion.2
  137.1 4.3 %collective-permute-start.18 = (bf16[8,64,1024]{2,1,0:T(8,128)(2,1)S(1)}, bf16[8,64,1024]{2,1,0:T(8,128)(2,1)S(1)}, u32[]{:S(2)}, u32[]{:S(2)}) collective-permute-start(bf16[8,64,1024]{2,1,0:T(8,128)(2,1)S(1)} %dynamic-slice_bitcast_fusion), channel_id=1, source_target_pairs={{0,8},{8,0},{1,9},{9,1},{2,10},{10,2},{3,11},{11,3},{4,12},{12,4},... | collective-permute-start | bytes 3145736 | tf_op jit(solution)/shard_map/ppermute | solution.py:50
  141.4 2.4 convolution_convert_fusion.1
  144.2 3.1 collective-permute-start.16
  147.2 3.3 %fusion.2 = (f32[1024]{0:T(1024)S(1)}, bf16[512,1024]{1,0:T(8,128)(2,1)}) fusion(bf16[128,1024]{1,0:T(8,128)(2,1)} %collective-permute-done.13, bf16[128,1024]{1,0:T(8,128)(2,1)} %collective-permute-done.12, bf16[128,1024]{1,0:T(8,128)(2,1)S(1)} %collective-permute-done.11, bf16[128,1024]{1,0:T(8,128)(2,1)} %bitcast.32, ...), kind=kOutput, calls=%fused_computation.13 | convolution fusion | flops 1079507968 | bytes 5246976 | tf_op jit(solution)/shard_map/dot_general | solution.py:35
  150.6 3.1 %collective-permute-done.14 = bf16[128,1024]{1,0:T(8,128)(2,1)S(1)} collective-permute-done((bf16[128,1024]{1,0:T(8,128)(2,1)S(1)}, bf16[128,1024]{1,0:T(8,128)(2,1)S(1)}, u32[]{:S(2)}, u32[]{:S(2)}) %collective-permute-start.14) | collective-permute-done | bytes 262176 | tf_op jit(solution)/shard_map/ppermute | solution.py:76
  153.7 3.7 %collective-permute-done.15 = bf16[128,1024]{1,0:T(8,128)(2,1)S(1)} collective-permute-done((bf16[128,1024]{1,0:T(8,128)(2,1)S(1)}, bf16[128,1024]{1,0:T(8,128)(2,1)S(1)}, u32[]{:S(2)}, u32[]{:S(2)}) %collective-permute-start.15) | collective-permute-done | bytes 262176 | tf_op jit(solution)/shard_map/ppermute | solution.py:76
  160.8 1.6 convolution_convert_fusion.2
  164.7 2.3 collective-permute-start.23
  168.2 2.5 collective-permute-start.19
  171.2 1.8 collective-permute-start.20
  175.8 3.7 %all-to-all-start.2 = ((bf16[8,128,128]{2,1,0:T(8,128)(2,1)}), bf16[8,128,128]{2,1,0:T(8,128)(2,1)S(1)}, u32[]{:S(2)}, u32[]{:S(2)}) async-start(bf16[8,128,128]{2,1,0:T(8,128)(2,1)} %bitcast.244), calls=%async_computation.2 | async-start | bytes 524288 | tf_op jit(solution)/shard_map/all_to_all | solution.py:54
  179.4 4.4 %collective-permute-done.19 = bf16[2,128,1024]{2,1,0:T(8,128)(2,1)} collective-permute-done((bf16[2,128,1024]{2,1,0:T(8,128)(2,1)}, bf16[2,128,1024]{2,1,0:T(8,128)(2,1)}, u32[]{:S(2)}, u32[]{:S(2)}) %collective-permute-start.19) | collective-permute-done | bytes 524320 | tf_op jit(solution)/shard_map/ppermute | solution.py:76
  185.0 12.4 %collective-permute-done.20 = bf16[2,128,1024]{2,1,0:T(8,128)(2,1)} collective-permute-done((bf16[2,128,1024]{2,1,0:T(8,128)(2,1)}, bf16[2,128,1024]{2,1,0:T(8,128)(2,1)}, u32[]{:S(2)}, u32[]{:S(2)}) %collective-permute-start.20) | collective-permute-done | bytes 524320 | tf_op jit(solution)/shard_map/ppermute | solution.py:76
  197.4 1.6 fusion.41
  200.4 1.7 fusion.4
  203.2 2.2 collective-permute-start.26
  206.7 7.5 %shard_map.281 = bf16[1024,384]{1,0:T(8,128)(2,1)S(1)} custom-call(bf16[1024,384]{1,0:T(8,128)(2,1)S(1)} %copy-done.11, f32[8,1024]{1,0:T(8,128)S(1)} %get-tuple-element.56.lse_ref, bf16[1024,128]{1,0:T(8,128)(2,1)S(1)} %bitcast.247), custom_call_target="tpu_custom_call" | custom-call | flops 5368709120 | bytes 2097152 | tf_op jit(solution)/shard_map/pallas_call | solution.py:278
  214.3 2.7 collective-permute-done.25
  218.0 4.3 %fusion.55 = (bf16[1024]{0:T(1024)(128)(2,1)S(1)}, bf16[1024]{0:T(1024)(128)(2,1)S(1)}, bf16[1024,1024]{1,0:T(8,128)(2,1)}, bf16[1024,1024]{1,0:T(8,128)(2,1)S(1)}) fusion(f32[1024]{0:T(1024)S(1)} %get-tuple-element.145, f32[1024]{0:T(1024)S(1)} %get-tuple-element.143, bf16[8,184,1024]{2,1,0:T(8,128)(2,1)} %all-to-all-done, ...), kind=kOutput, calls=%fused_computation.193 | convolution fusion | flops 815790080 | bytes 7884800 | tf_op jit(solution)/shard_map/dot_general | solution.py:39
  223.4 2.7 collective-permute-start.27
  226.6 3.7 %collective-permute-done.27 = bf16[128,1024]{1,0:T(8,128)(2,1)} collective-permute-done((bf16[128,1024]{1,0:T(8,128)(2,1)S(1)}, bf16[128,1024]{1,0:T(8,128)(2,1)}, u32[]{:S(2)}, u32[]{:S(2)}) %collective-permute-start.27) | collective-permute-done | bytes 262176 | tf_op jit(solution)/shard_map/ppermute | solution.py:50
  232.0 3.6 %collective-permute-start.28 = (bf16[8,4,16,512]{3,2,1,0:T(8,128)(2,1)S(1)}, bf16[8,4,16,512]{3,2,1,0:T(8,128)(2,1)S(1)}, u32[]{:S(2)}, u32[]{:S(2)}) collective-permute-start(bf16[8,4,16,512]{3,2,1,0:T(8,128)(2,1)S(1)} %dynamic-slice_bitcast_fusion.2), channel_id=1, source_target_pairs={{0,8},{8,0},{1,9},{9,1},{2,10},{10,2},{3,11},{11,3},{4,12},{12,4},... | collective-permute-start | bytes 1572872 | tf_op jit(solution)/shard_map/ppermute | solution.py:50
  235.6 1.5 collective-permute-done.28
  238.3 1.8 collective-permute-start.31
  240.2 4.5 %all-to-all-start.3 = ((bf16[8,128,1024]{2,1,0:T(8,128)(2,1)}), bf16[8,128,1024]{2,1,0:T(8,128)(2,1)}, u32[]{:S(2)}, u32[]{:S(2)}) async-start(bf16[8,128,1024]{2,1,0:T(8,128)(2,1)} %bitcast.262), calls=%async_computation.3 | async-start | bytes 4194304 | tf_op jit(solution)/shard_map/all_to_all | solution.py:54
  245.8 2.3 collective-permute-start.44
  248.1 1.8 collective-permute-start.43
  250.0 3.1 collective-permute-done.45.refs_3_
  253.1 5.8 %collective-permute-done.44.refs_2_ = bf16[128,1024]{1,0:T(8,128)(2,1)S(1)} collective-permute-done((bf16[128,1024]{1,0:T(8,128)(2,1)S(1)}, bf16[128,1024]{1,0:T(8,128)(2,1)S(1)}, u32[]{:S(2)}, u32[]{:S(2)}) %collective-permute-start.44) | collective-permute-done | bytes 262176 | tf_op jit(solution)/shard_map/ppermute | solution.py:72
  259.5 1.7 collective-permute-start.46
  265.5 1.7 collective-permute-start.33
  267.3 2.6 collective-permute-start.35
  269.9 3.0 shard_map.283
  272.9 5.0 %collective-permute-done.33 = bf16[128,1024]{1,0:T(8,128)(2,1)S(1)} collective-permute-done((bf16[128,1024]{1,0:T(8,128)(2,1)S(1)}, bf16[128,1024]{1,0:T(8,128)(2,1)S(1)}, u32[]{:S(2)}, u32[]{:S(2)}) %collective-permute-start.33) | collective-permute-done | bytes 262176 | tf_op jit(solution)/shard_map/ppermute | solution.py:76
  277.9 1.9 fusion.43
  280.7 5.0 %all-to-all-start.4 = ((bf16[8,16,1536]{2,1,0:T(8,128)(2,1)}), bf16[8,16,1536]{2,1,0:T(8,128)(2,1)S(1)}, u32[]{:S(2)}, u32[]{:S(2)}) async-start(bf16[8,16,1536]{2,1,0:T(8,128)(2,1)} %add_convert_fusion.4), calls=%async_computation.4 | async-start | bytes 786432 | tf_op jit(solution)/shard_map/all_to_all | solution.py:54
  285.6 2.0 convert_reduce_fusion
  288.2 4.3 %all-to-all-done.4 = bf16[8,16,1536]{2,1,0:T(8,128)(2,1)S(1)} async-done(((bf16[8,16,1536]{2,1,0:T(8,128)(2,1)}), bf16[8,16,1536]{2,1,0:T(8,128)(2,1)S(1)}, u32[]{:S(2)}, u32[]{:S(2)}) %all-to-all-start.4) | async-done | bytes 393248 | tf_op jit(solution)/shard_map/all_to_all | solution.py:54
  293.4 2.1 collective-permute-start.37
  296.5 3.9 %collective-permute-start.39 = (bf16[16,4224]{1,0:T(8,128)(2,1)S(1)}, bf16[16,4224]{1,0:T(8,128)(2,1)S(1)}, u32[]{:S(2)}, u32[]{:S(2)}) collective-permute-start(bf16[16,4224]{1,0:T(8,128)(2,1)S(1)} %pad_maximum_fusion.10.refs_0_), channel_id=1, source_target_pairs={{0,8},{8,0},{1,9},{9,1},{2,10},{10,2},{3,11},{11,3},{4,12},{12,4},... | collective-permute-start | bytes 405512 | tf_op jit(solution)/shard_map/ppermute | solution.py:50
  301.8 1.7 collective-permute-start.41
  304.1 1.9 fusion.42
  306.1 2.0 shard_map.282
  (241 shorter events, 60.2 us)
Async XLA Ops:
  4.1 10.7 %collective-permute-start = (bf16[192,1024]{1,0:T(8,128)(2,1)S(1)}, bf16[192,1024]{1,0:T(8,128)(2,1)}, u32[]{:S(2)}, u32[]{:S(2)}) collective-permute-start(bf16[192,1024]{1,0:T(8,128)(2,1)S(1)} %pad_maximum_fusion.5), channel_id=1, source_target_pairs={{0,1},{1,0},{2,3},{3,2},{4,5},{5,4},{6,7},{7,6},{8,9},{9,8},{10,11... | collective-permute-start | bytes 1179656 | tf_op jit(solution)/shard_map/ppermute | solution.py:50
  14.8 41.7 %all-to-all-start = ((bf16[8,184,1024]{2,1,0:T(8,128)(2,1)}), bf16[8,184,1024]{2,1,0:T(8,128)(2,1)}, u32[]{:S(2)}, u32[]{:S(2)}) async-start(bf16[8,184,1024]{2,1,0:T(8,128)(2,1)} %pad_maximum_fusion), calls=%async_computation | async-start | bytes 6029312 | tf_op jit(solution)/shard_map/all_to_all | solution.py:54
  22.4 52.2 %collective-permute-start.3 = (bf16[2,192,1024]{2,1,0:T(8,128)(2,1)S(1)}, bf16[2,192,1024]{2,1,0:T(8,128)(2,1)S(1)}, u32[]{:S(2)}, u32[]{:S(2)}) collective-permute-start(bf16[2,192,1024]{2,1,0:T(8,128)(2,1)S(1)} %pad_maximum_fusion.4.refs_0_), channel_id=1, source_target_pairs={{6,0},{0,2},{2,4},{4,6},{7,1},{1,3},{3,5},{5,7},{14,8},{8,10},{10,... | collective-permute-start | bytes 2359304 | tf_op jit(solution)/shard_map/ppermute | solution.py:72
  23.9 65.3 %collective-permute-start.2 = (bf16[2,192,1024]{2,1,0:T(8,128)(2,1)S(1)}, bf16[2,192,1024]{2,1,0:T(8,128)(2,1)S(1)}, u32[]{:S(2)}, u32[]{:S(2)}) collective-permute-start(bf16[2,192,1024]{2,1,0:T(8,128)(2,1)S(1)} %pad_maximum_fusion.4.refs_0_), channel_id=1, source_target_pairs={{4,0},{6,2},{0,4},{2,6},{5,1},{7,3},{1,5},{3,7},{12,8},{14,10},{8,... | collective-permute-start | bytes 2359304 | tf_op jit(solution)/shard_map/ppermute | solution.py:72
  26.3 62.9 %collective-permute-start.1 = (bf16[2,192,1024]{2,1,0:T(8,128)(2,1)S(1)}, bf16[2,192,1024]{2,1,0:T(8,128)(2,1)}, u32[]{:S(2)}, u32[]{:S(2)}) collective-permute-start(bf16[2,192,1024]{2,1,0:T(8,128)(2,1)S(1)} %pad_maximum_fusion.4.refs_0_), channel_id=1, source_target_pairs={{2,0},{4,2},{6,4},{0,6},{3,1},{5,3},{7,5},{1,7},{10,8},{12,10},{14... | collective-permute-start | bytes 2359304 | tf_op jit(solution)/shard_map/ppermute | solution.py:72
  67.9 6.7 %copy-start.10 = (bf16[1024,384]{1,0:T(8,128)(2,1)}, bf16[1024,384]{1,0:T(8,128)(2,1)S(1)}, u32[]{:S(2)}) copy-start(bf16[1024,384]{1,0:T(8,128)(2,1)S(1)} %add_convert_fusion.3.mixed_ref) | copy-start | bytes 2359300
  74.6 27.6 %copy-start.2 = (bf16[2,192,1024]{2,1,0:T(8,128)(2,1)}, bf16[2,192,1024]{2,1,0:T(8,128)(2,1)S(1)}, u32[]{:S(2)}) copy-start(bf16[2,192,1024]{2,1,0:T(8,128)(2,1)S(1)} %collective-permute-done.3.refs_3_) | copy-start | bytes 2359300
  89.2 10.6 %collective-permute-start.4 = (bf16[2,192,1024]{2,1,0:T(8,128)(2,1)S(1)}, bf16[2,192,1024]{2,1,0:T(8,128)(2,1)}, u32[]{:S(2)}, u32[]{:S(2)}) collective-permute-start(bf16[2,192,1024]{2,1,0:T(8,128)(2,1)S(1)} %pad_maximum_fusion.4.refs_0_), channel_id=1, source_target_pairs={{0,8},{8,0},{1,9},{9,1},{2,10},{10,2},{3,11},{11,3},{4,12},{12,4},... | collective-permute-start | bytes 2359304 | tf_op jit(solution)/shard_map/ppermute | solution.py:50
  91.9 10.3 %collective-permute-start.5 = (bf16[2,192,1024]{2,1,0:T(8,128)(2,1)}, bf16[2,192,1024]{2,1,0:T(8,128)(2,1)}, u32[]{:S(2)}, u32[]{:S(2)}) collective-permute-start(bf16[2,192,1024]{2,1,0:T(8,128)(2,1)} %collective-permute-done.1.refs_1_), channel_id=1, source_target_pairs={{0,8},{8,0},{1,9},{9,1},{2,10},{10,2},{3,11},{11,3},{4,12},{12,4},... | collective-permute-start | bytes 2359304 | tf_op jit(solution)/shard_map/ppermute | solution.py:50
  91.9 10.3 %collective-permute-start.6 = (bf16[2,192,1024]{2,1,0:T(8,128)(2,1)S(1)}, bf16[2,192,1024]{2,1,0:T(8,128)(2,1)}, u32[]{:S(2)}, u32[]{:S(2)}) collective-permute-start(bf16[2,192,1024]{2,1,0:T(8,128)(2,1)S(1)} %collective-permute-done.2.refs_2_), channel_id=1, source_target_pairs={{0,8},{8,0},{1,9},{9,1},{2,10},{10,2},{3,11},{11,3},{4,12},{12,4},... | collective-permute-start | bytes 2359304 | tf_op jit(solution)/shard_map/ppermute | solution.py:50
  93.3 8.9 %collective-permute-start.7 = (bf16[2,192,1024]{2,1,0:T(8,128)(2,1)S(1)}, bf16[2,192,1024]{2,1,0:T(8,128)(2,1)}, u32[]{:S(2)}, u32[]{:S(2)}) collective-permute-start(bf16[2,192,1024]{2,1,0:T(8,128)(2,1)S(1)} %collective-permute-done.3.refs_3_), channel_id=1, source_target_pairs={{0,8},{8,0},{1,9},{9,1},{2,10},{10,2},{3,11},{11,3},{4,12},{12,4},... | collective-permute-start | bytes 2359304 | tf_op jit(solution)/shard_map/ppermute | solution.py:50
  94.2 15.5 %all-to-all-start.1 = ((bf16[8,128,128]{1,2,0:T(8,128)(2,1)}), bf16[8,128,128]{1,2,0:T(8,128)(2,1)}, u32[]{:S(2)}, u32[]{:S(2)}) async-start(bf16[8,128,128]{1,2,0:T(8,128)(2,1)} %copy.49), calls=%async_computation.1 | async-start | bytes 524288 | tf_op jit(solution)/shard_map/all_to_all | solution.py:54
  98.4 32.9 %collective-permute-start.13 = (bf16[128,1024]{1,0:T(8,128)(2,1)}, bf16[128,1024]{1,0:T(8,128)(2,1)}, u32[]{:S(2)}, u32[]{:S(2)}) collective-permute-start(bf16[128,1024]{1,0:T(8,128)(2,1)} %bitcast.32), channel_id=1, source_target_pairs={{48,0},{0,16},{16,32},{32,48},{49,1},{1,17},{17,33},{33,49},{50,2}... | collective-permute-start | bytes 786440 | tf_op jit(solution)/shard_map/ppermute | solution.py:72
  99.7 31.6 %collective-permute-start.12 = (bf16[128,1024]{1,0:T(8,128)(2,1)}, bf16[128,1024]{1,0:T(8,128)(2,1)}, u32[]{:S(2)}, u32[]{:S(2)}) collective-permute-start(bf16[128,1024]{1,0:T(8,128)(2,1)} %bitcast.32), channel_id=1, source_target_pairs={{32,0},{48,16},{0,32},{16,48},{33,1},{49,17},{1,33},{17,49},{34,2}... | collective-permute-start | bytes 786440 | tf_op jit(solution)/shard_map/ppermute | solution.py:72
  109.7 16.1 %copy-start.9 = (bf16[1024,1024]{1,0:T(8,128)(2,1)S(1)}, bf16[1024,1024]{1,0:T(8,128)(2,1)}, u32[]{:S(2)}) copy-start(bf16[1024,1024]{1,0:T(8,128)(2,1)} %copy-done.8) | copy-start | bytes 6291460
  111.7 8.1 %collective-permute-start.10 = (bf16[128,1024]{1,0:T(8,128)(2,1)S(1)}, bf16[128,1024]{1,0:T(8,128)(2,1)S(1)}, u32[]{:S(2)}, u32[]{:S(2)}) collective-permute-start(bf16[128,1024]{1,0:T(8,128)(2,1)S(1)} %add_convert_fusion.7), channel_id=1, source_target_pairs={{48,0},{0,16},{16,32},{32,48},{49,1},{1,17},{17,33},{33,49},{50,2}... | collective-permute-start | bytes 786440 | tf_op jit(solution)/shard_map/ppermute | solution.py:72
  111.8 13.1 %collective-permute-start.9 = (bf16[128,1024]{1,0:T(8,128)(2,1)S(1)}, bf16[128,1024]{1,0:T(8,128)(2,1)S(1)}, u32[]{:S(2)}, u32[]{:S(2)}) collective-permute-start(bf16[128,1024]{1,0:T(8,128)(2,1)S(1)} %add_convert_fusion.7), channel_id=1, source_target_pairs={{32,0},{48,16},{0,32},{16,48},{33,1},{49,17},{1,33},{17,49},{34,2}... | collective-permute-start | bytes 786440 | tf_op jit(solution)/shard_map/ppermute | solution.py:72
  114.2 11.6 %collective-permute-start.8 = (bf16[128,1024]{1,0:T(8,128)(2,1)S(1)}, bf16[128,1024]{1,0:T(8,128)(2,1)S(1)}, u32[]{:S(2)}, u32[]{:S(2)}) collective-permute-start(bf16[128,1024]{1,0:T(8,128)(2,1)S(1)} %add_convert_fusion.7), channel_id=1, source_target_pairs={{16,0},{32,16},{48,32},{0,48},{17,1},{33,17},{49,33},{1,49},{18,2}... | collective-permute-start | bytes 786440 | tf_op jit(solution)/shard_map/ppermute | solution.py:72
  119.9 11.4 %collective-permute-start.11 = (bf16[128,1024]{1,0:T(8,128)(2,1)}, bf16[128,1024]{1,0:T(8,128)(2,1)S(1)}, u32[]{:S(2)}, u32[]{:S(2)}) collective-permute-start(bf16[128,1024]{1,0:T(8,128)(2,1)} %bitcast.32), channel_id=1, source_target_pairs={{16,0},{32,16},{48,32},{0,48},{17,1},{33,17},{49,33},{1,49},{18,2}... | collective-permute-start | bytes 786440 | tf_op jit(solution)/shard_map/ppermute | solution.py:72
  137.1 20.4 %collective-permute-start.18 = (bf16[8,64,1024]{2,1,0:T(8,128)(2,1)S(1)}, bf16[8,64,1024]{2,1,0:T(8,128)(2,1)S(1)}, u32[]{:S(2)}, u32[]{:S(2)}) collective-permute-start(bf16[8,64,1024]{2,1,0:T(8,128)(2,1)S(1)} %dynamic-slice_bitcast_fusion), channel_id=1, source_target_pairs={{0,8},{8,0},{1,9},{9,1},{2,10},{10,2},{3,11},{11,3},{4,12},{12,4},... | collective-permute-start | bytes 3145736 | tf_op jit(solution)/shard_map/ppermute | solution.py:50
  143.9 14.1 %collective-permute-start.17 = (bf16[8,64,1024]{2,1,0:T(8,128)(2,1)S(1)}, bf16[8,64,1024]{2,1,0:T(8,128)(2,1)S(1)}, u32[]{:S(2)}, u32[]{:S(2)}) collective-permute-start(bf16[8,64,1024]{2,1,0:T(8,128)(2,1)S(1)} %dynamic-slice_bitcast_fusion.1), channel_id=1, source_target_pairs={{0,8},{8,0},{1,9},{9,1},{2,10},{10,2},{3,11},{11,3},{4,12},{12,4},... | collective-permute-start | bytes 3145736 | tf_op jit(solution)/shard_map/ppermute | solution.py:50
  144.1 9.6 %collective-permute-start.14 = (bf16[128,1024]{1,0:T(8,128)(2,1)S(1)}, bf16[128,1024]{1,0:T(8,128)(2,1)S(1)}, u32[]{:S(2)}, u32[]{:S(2)}) collective-permute-start(bf16[128,1024]{1,0:T(8,128)(2,1)S(1)} %get-tuple-element.108), channel_id=1, source_target_pairs={{0,16},{16,32},{32,48},{48,0},{1,17},{17,33},{33,49},{49,1},{2,18}... | collective-permute-start | bytes 786440 | tf_op jit(solution)/shard_map/ppermute | solution.py:76
  144.2 9.5 %collective-permute-start.16 = (bf16[128,1024]{1,0:T(8,128)(2,1)S(1)}, bf16[128,1024]{1,0:T(8,128)(2,1)S(1)}, u32[]{:S(2)}, u32[]{:S(2)}) collective-permute-start(bf16[128,1024]{1,0:T(8,128)(2,1)S(1)} %get-tuple-element.109), channel_id=1, source_target_pairs={{0,48},{16,0},{32,16},{48,32},{1,49},{17,1},{33,17},{49,33},{2,50}... | collective-permute-start | bytes 786440 | tf_op jit(solution)/shard_map/ppermute | solution.py:76
  147.2 10.2 %collective-permute-start.15 = (bf16[128,1024]{1,0:T(8,128)(2,1)S(1)}, bf16[128,1024]{1,0:T(8,128)(2,1)S(1)}, u32[]{:S(2)}, u32[]{:S(2)}) collective-permute-start(bf16[128,1024]{1,0:T(8,128)(2,1)S(1)} %get-tuple-element.110), channel_id=1, source_target_pairs={{0,32},{16,48},{32,0},{48,16},{1,33},{17,49},{33,1},{49,17},{2,34}... | collective-permute-start | bytes 786440 | tf_op jit(solution)/shard_map/ppermute | solution.py:76
  158.9 8.1 %copy-start.12 = (bf16[8,2,64,1024]{3,2,1,0:T(8,128)(2,1)}, bf16[8,2,64,1024]{3,2,1,0:T(8,128)(2,1)S(1)}, u32[]{:S(2)}) copy-start(bf16[8,2,64,1024]{3,2,1,0:T(8,128)(2,1)S(1)} %copy.52) | copy-start | bytes 6291460
  159.5 13.5 %copy-start.13 = (f32[128,1024]{1,0:T(8,128)}, f32[128,1024]{1,0:T(8,128)S(1)}, u32[]{:S(2)}) copy-start(f32[128,1024]{1,0:T(8,128)S(1)} %get-tuple-element.88) | copy-start | bytes 1572868
  164.7 35.6 %collective-permute-start.23 = (bf16[8,4,16,1024]{3,2,0,1:T(8,128)(2,1)}, bf16[8,4,16,1024]{3,2,0,1:T(8,128)(2,1)}, u32[]{:S(2)}, u32[]{:S(2)}) collective-permute-start(bf16[8,4,16,1024]{3,2,0,1:T(8,128)(2,1)} %bitcast.242), channel_id=1, source_target_pairs={{0,8},{8,0},{1,9},{9,1},{2,10},{10,2},{3,11},{11,3},{4,12},{12,4},... | collective-permute-start | bytes 3145736 | tf_op jit(solution)/shard_map/ppermute | solution.py:50
  168.2 15.6 %collective-permute-start.19 = (bf16[2,128,1024]{2,1,0:T(8,128)(2,1)}, bf16[2,128,1024]{2,1,0:T(8,128)(2,1)}, u32[]{:S(2)}, u32[]{:S(2)}) collective-permute-start(bf16[2,128,1024]{2,1,0:T(8,128)(2,1)} %get-tuple-element.99), channel_id=1, source_target_pairs={{0,2},{2,4},{4,6},{6,0},{1,3},{3,5},{5,7},{7,1},{8,10},{10,12},{12... | collective-permute-start | bytes 1572872 | tf_op jit(solution)/shard_map/ppermute | solution.py:76
  170.8 14.3 %collective-permute-start.21 = (bf16[2,128,1024]{2,1,0:T(8,128)(2,1)}, bf16[2,128,1024]{2,1,0:T(8,128)(2,1)}, u32[]{:S(2)}, u32[]{:S(2)}) collective-permute-start(bf16[2,128,1024]{2,1,0:T(8,128)(2,1)} %get-tuple-element.100), channel_id=1, source_target_pairs={{0,6},{2,0},{4,2},{6,4},{1,7},{3,1},{5,3},{7,5},{8,14},{10,8},{12,... | collective-permute-start | bytes 1572872 | tf_op jit(solution)/shard_map/ppermute | solution.py:76
  171.2 26.2 %collective-permute-start.20 = (bf16[2,128,1024]{2,1,0:T(8,128)(2,1)}, bf16[2,128,1024]{2,1,0:T(8,128)(2,1)}, u32[]{:S(2)}, u32[]{:S(2)}) collective-permute-start(bf16[2,128,1024]{2,1,0:T(8,128)(2,1)} %get-tuple-element.101), channel_id=1, source_target_pairs={{0,4},{2,6},{4,0},{6,2},{1,5},{3,7},{5,1},{7,3},{8,12},{10,14},{12... | collective-permute-start | bytes 1572872 | tf_op jit(solution)/shard_map/ppermute | solution.py:76
  175.0 25.4 %copy-start.16 = (bf16[8,1,4,16,1024]{4,3,2,1,0:T(8,128)(2,1)S(1)}, bf16[8,1,4,16,1024]{4,3,2,1,0:T(8,128)(2,1)}, u32[]{:S(2)}) copy-start(bf16[8,1,4,16,1024]{4,3,2,1,0:T(8,128)(2,1)} %get-tuple-element.97) | copy-start | bytes 3145732
  175.8 23.3 %all-to-all-start.2 = ((bf16[8,128,128]{2,1,0:T(8,128)(2,1)}), bf16[8,128,128]{2,1,0:T(8,128)(2,1)S(1)}, u32[]{:S(2)}, u32[]{:S(2)}) async-start(bf16[8,128,128]{2,1,0:T(8,128)(2,1)} %bitcast.244), calls=%async_computation.2 | async-start | bytes 524288 | tf_op jit(solution)/shard_map/all_to_all | solution.py:54
  199.1 15.1 %collective-permute-start.22 = (bf16[128,1024]{1,0:T(8,128)(2,1)S(1)}, bf16[128,1024]{1,0:T(8,128)(2,1)S(1)}, u32[]{:S(2)}, u32[]{:S(2)}) collective-permute-start(bf16[128,1024]{1,0:T(8,128)(2,1)S(1)} %dynamic-slice_bitcast_fusion.9), channel_id=1, source_target_pairs={{0,1},{1,0},{2,3},{3,2},{4,5},{5,4},{6,7},{7,6},{8,9},{9,8},{10,11... | collective-permute-start | bytes 786440 | tf_op jit(solution)/shard_map/ppermute | solution.py:50
  202.1 12.2 %collective-permute-start.24 = (bf16[8,16,1024]{2,1,0:T(8,128)(2,1)S(1)}, bf16[8,16,1024]{2,1,0:T(8,128)(2,1)S(1)}, u32[]{:S(2)}, u32[]{:S(2)}) collective-permute-start(bf16[8,16,1024]{2,1,0:T(8,128)(2,1)S(1)} %get-tuple-element.105), channel_id=1, source_target_pairs={{0,16},{16,32},{32,48},{48,0},{1,17},{17,33},{33,49},{49,1},{2,18}... | collective-permute-start | bytes 786440 | tf_op jit(solution)/shard_map/ppermute | solution.py:76
  203.2 11.1 %collective-permute-start.26 = (bf16[8,16,1024]{2,1,0:T(8,128)(2,1)S(1)}, bf16[8,16,1024]{2,1,0:T(8,128)(2,1)S(1)}, u32[]{:S(2)}, u32[]{:S(2)}) collective-permute-start(bf16[8,16,1024]{2,1,0:T(8,128)(2,1)S(1)} %get-tuple-element.106), channel_id=1, source_target_pairs={{0,48},{16,0},{32,16},{48,32},{1,49},{17,1},{33,17},{49,33},{2,50}... | collective-permute-start | bytes 786440 | tf_op jit(solution)/shard_map/ppermute | solution.py:76
  205.4 11.6 %collective-permute-start.25 = (bf16[8,16,1024]{2,1,0:T(8,128)(2,1)S(1)}, bf16[8,16,1024]{2,1,0:T(8,128)(2,1)S(1)}, u32[]{:S(2)}, u32[]{:S(2)}) collective-permute-start(bf16[8,16,1024]{2,1,0:T(8,128)(2,1)S(1)} %get-tuple-element.107), channel_id=1, source_target_pairs={{0,32},{16,48},{32,0},{48,16},{1,33},{17,49},{33,1},{49,17},{2,34}... | collective-permute-start | bytes 786440 | tf_op jit(solution)/shard_map/ppermute | solution.py:76
  223.4 6.9 %collective-permute-start.27 = (bf16[128,1024]{1,0:T(8,128)(2,1)S(1)}, bf16[128,1024]{1,0:T(8,128)(2,1)}, u32[]{:S(2)}, u32[]{:S(2)}) collective-permute-start(bf16[128,1024]{1,0:T(8,128)(2,1)S(1)} %fusion.39), channel_id=1, source_target_pairs={{0,64},{64,0},{1,65},{65,1},{2,66},{66,2},{3,67},{67,3},{4,68},{68... | collective-permute-start | bytes 786440 | tf_op jit(solution)/shard_map/ppermute | solution.py:50
  232.0 5.1 %collective-permute-start.28 = (bf16[8,4,16,512]{3,2,1,0:T(8,128)(2,1)S(1)}, bf16[8,4,16,512]{3,2,1,0:T(8,128)(2,1)S(1)}, u32[]{:S(2)}, u32[]{:S(2)}) collective-permute-start(bf16[8,4,16,512]{3,2,1,0:T(8,128)(2,1)S(1)} %dynamic-slice_bitcast_fusion.2), channel_id=1, source_target_pairs={{0,8},{8,0},{1,9},{9,1},{2,10},{10,2},{3,11},{11,3},{4,12},{12,4},... | collective-permute-start | bytes 1572872 | tf_op jit(solution)/shard_map/ppermute | solution.py:50
  237.3 10.7 %collective-permute-start.29 = (bf16[8,16,512]{2,1,0:T(8,128)(2,1)S(1)}, bf16[8,16,512]{2,1,0:T(8,128)(2,1)S(1)}, u32[]{:S(2)}, u32[]{:S(2)}) collective-permute-start(bf16[8,16,512]{2,1,0:T(8,128)(2,1)S(1)} %get-tuple-element.113), channel_id=1, source_target_pairs={{0,16},{16,32},{32,48},{48,0},{1,17},{17,33},{33,49},{49,1},{2,18}... | collective-permute-start | bytes 393224 | tf_op jit(solution)/shard_map/ppermute | solution.py:76
  238.3 11.6 %collective-permute-start.31 = (bf16[8,16,512]{2,1,0:T(8,128)(2,1)S(1)}, bf16[8,16,512]{2,1,0:T(8,128)(2,1)S(1)}, u32[]{:S(2)}, u32[]{:S(2)}) collective-permute-start(bf16[8,16,512]{2,1,0:T(8,128)(2,1)S(1)} %get-tuple-element.114), channel_id=1, source_target_pairs={{0,48},{16,0},{32,16},{48,32},{1,49},{17,1},{33,17},{49,33},{2,50}... | collective-permute-start | bytes 393224 | tf_op jit(solution)/shard_map/ppermute | solution.py:76
  240.1 9.8 %collective-permute-start.30 = (bf16[8,16,512]{2,1,0:T(8,128)(2,1)S(1)}, bf16[8,16,512]{2,1,0:T(8,128)(2,1)S(1)}, u32[]{:S(2)}, u32[]{:S(2)}) collective-permute-start(bf16[8,16,512]{2,1,0:T(8,128)(2,1)S(1)} %get-tuple-element.115), channel_id=1, source_target_pairs={{0,32},{16,48},{32,0},{48,16},{1,33},{17,49},{33,1},{49,17},{2,34}... | collective-permute-start | bytes 393224 | tf_op jit(solution)/shard_map/ppermute | solution.py:76
  240.2 9.8 %copy-start.17 = (bf16[8,16,1024]{2,1,0:T(8,128)(2,1)S(1)}, bf16[8,16,1024]{2,1,0:T(8,128)(2,1)}, u32[]{:S(2)}) copy-start(bf16[8,16,1024]{2,1,0:T(8,128)(2,1)} %fusion.38) | copy-start | bytes 786436
  240.2 40.5 %all-to-all-start.3 = ((bf16[8,128,1024]{2,1,0:T(8,128)(2,1)}), bf16[8,128,1024]{2,1,0:T(8,128)(2,1)}, u32[]{:S(2)}, u32[]{:S(2)}) async-start(bf16[8,128,1024]{2,1,0:T(8,128)(2,1)} %bitcast.262), calls=%async_computation.3 | async-start | bytes 4194304 | tf_op jit(solution)/shard_map/all_to_all | solution.py:54
  244.7 8.5 %collective-permute-start.45 = (bf16[128,1024]{1,0:T(8,128)(2,1)S(1)}, bf16[128,1024]{1,0:T(8,128)(2,1)S(1)}, u32[]{:S(2)}, u32[]{:S(2)}) collective-permute-start(bf16[128,1024]{1,0:T(8,128)(2,1)S(1)} %add_convert_fusion.6.refs_0_), channel_id=1, source_target_pairs={{48,0},{0,16},{16,32},{32,48},{49,1},{1,17},{17,33},{33,49},{50,2}... | collective-permute-start | bytes 786440 | tf_op jit(solution)/shard_map/ppermute | solution.py:72
  245.8 13.1 %collective-permute-start.44 = (bf16[128,1024]{1,0:T(8,128)(2,1)S(1)}, bf16[128,1024]{1,0:T(8,128)(2,1)S(1)}, u32[]{:S(2)}, u32[]{:S(2)}) collective-permute-start(bf16[128,1024]{1,0:T(8,128)(2,1)S(1)} %add_convert_fusion.6.refs_0_), channel_id=1, source_target_pairs={{32,0},{48,16},{0,32},{16,48},{33,1},{49,17},{1,33},{17,49},{34,2}... | collective-permute-start | bytes 786440 | tf_op jit(solution)/shard_map/ppermute | solution.py:72
  248.1 11.4 %collective-permute-start.43 = (bf16[128,1024]{1,0:T(8,128)(2,1)S(1)}, bf16[128,1024]{1,0:T(8,128)(2,1)S(1)}, u32[]{:S(2)}, u32[]{:S(2)}) collective-permute-start(bf16[128,1024]{1,0:T(8,128)(2,1)S(1)} %add_convert_fusion.6.refs_0_), channel_id=1, source_target_pairs={{16,0},{32,16},{48,32},{0,48},{17,1},{33,17},{49,33},{1,49},{18,2}... | collective-permute-start | bytes 786440 | tf_op jit(solution)/shard_map/ppermute | solution.py:72
  259.5 4.8 %collective-permute-start.46 = (bf16[128,1024]{1,0:T(8,128)(2,1)S(1)}, bf16[128,1024]{1,0:T(8,128)(2,1)S(1)}, u32[]{:S(2)}, u32[]{:S(2)}) collective-permute-start(bf16[128,1024]{1,0:T(8,128)(2,1)S(1)} %add_convert_fusion.6.refs_0_), channel_id=1, source_target_pairs={{0,8},{8,0},{1,9},{9,1},{2,10},{10,2},{3,11},{11,3},{4,12},{12,4},... | collective-permute-start | bytes 786440 | tf_op jit(solution)/shard_map/ppermute | solution.py:50
  261.1 4.4 %collective-permute-start.47 = (bf16[128,1024]{1,0:T(8,128)(2,1)S(1)}, bf16[128,1024]{1,0:T(8,128)(2,1)S(1)}, u32[]{:S(2)}, u32[]{:S(2)}) collective-permute-start(bf16[128,1024]{1,0:T(8,128)(2,1)S(1)} %collective-permute-done.43.refs_1_), channel_id=1, source_target_pairs={{0,8},{8,0},{1,9},{9,1},{2,10},{10,2},{3,11},{11,3},{4,12},{12,4},... | collective-permute-start | bytes 786440 | tf_op jit(solution)/shard_map/ppermute | solution.py:50
  261.1 6.2 %collective-permute-start.48 = (bf16[128,1024]{1,0:T(8,128)(2,1)S(1)}, bf16[128,1024]{1,0:T(8,128)(2,1)S(1)}, u32[]{:S(2)}, u32[]{:S(2)}) collective-permute-start(bf16[128,1024]{1,0:T(8,128)(2,1)S(1)} %collective-permute-done.44.refs_2_), channel_id=1, source_target_pairs={{0,8},{8,0},{1,9},{9,1},{2,10},{10,2},{3,11},{11,3},{4,12},{12,4},... | collective-permute-start | bytes 786440 | tf_op jit(solution)/shard_map/ppermute | solution.py:50
  261.6 8.3 %collective-permute-start.49 = (bf16[128,1024]{1,0:T(8,128)(2,1)S(1)}, bf16[128,1024]{1,0:T(8,128)(2,1)S(1)}, u32[]{:S(2)}, u32[]{:S(2)}) collective-permute-start(bf16[128,1024]{1,0:T(8,128)(2,1)S(1)} %collective-permute-done.45.refs_3_), channel_id=1, source_target_pairs={{0,8},{8,0},{1,9},{9,1},{2,10},{10,2},{3,11},{11,3},{4,12},{12,4},... | collective-permute-start | bytes 786440 | tf_op jit(solution)/shard_map/ppermute | solution.py:50
  262.8 10.1 %collective-permute-start.32 = (bf16[128,1024]{1,0:T(8,128)(2,1)S(1)}, bf16[128,1024]{1,0:T(8,128)(2,1)S(1)}, u32[]{:S(2)}, u32[]{:S(2)}) collective-permute-start(bf16[128,1024]{1,0:T(8,128)(2,1)S(1)} %get-tuple-element.102), channel_id=1, source_target_pairs={{0,16},{16,32},{32,48},{48,0},{1,17},{17,33},{33,49},{49,1},{2,18}... | collective-permute-start | bytes 786440 | tf_op jit(solution)/shard_map/ppermute | solution.py:76
  264.3 8.7 %collective-permute-start.34 = (bf16[128,1024]{1,0:T(8,128)(2,1)S(1)}, bf16[128,1024]{1,0:T(8,128)(2,1)S(1)}, u32[]{:S(2)}, u32[]{:S(2)}) collective-permute-start(bf16[128,1024]{1,0:T(8,128)(2,1)S(1)} %get-tuple-element.103), channel_id=1, source_target_pairs={{0,48},{16,0},{32,16},{48,32},{1,49},{17,1},{33,17},{49,33},{2,50}... | collective-permute-start | bytes 786440 | tf_op jit(solution)/shard_map/ppermute | solution.py:76
  265.5 12.4 %collective-permute-start.33 = (bf16[128,1024]{1,0:T(8,128)(2,1)S(1)}, bf16[128,1024]{1,0:T(8,128)(2,1)S(1)}, u32[]{:S(2)}, u32[]{:S(2)}) collective-permute-start(bf16[128,1024]{1,0:T(8,128)(2,1)S(1)} %get-tuple-element.104), channel_id=1, source_target_pairs={{0,32},{16,48},{32,0},{48,16},{1,33},{17,49},{33,1},{49,17},{2,34}... | collective-permute-start | bytes 786440 | tf_op jit(solution)/shard_map/ppermute | solution.py:76
  267.3 12.5 %collective-permute-start.35 = (bf16[8,16,1536]{2,1,0:T(8,128)(2,1)S(1)}, bf16[8,16,1536]{2,1,0:T(8,128)(2,1)S(1)}, u32[]{:S(2)}, u32[]{:S(2)}) collective-permute-start(bf16[8,16,1536]{2,1,0:T(8,128)(2,1)S(1)} %pad_maximum_fusion.6), channel_id=1, source_target_pairs={{0,64},{64,0},{1,65},{65,1},{2,66},{66,2},{3,67},{67,3},{4,68},{68... | collective-permute-start | bytes 1179656 | tf_op jit(solution)/shard_map/ppermute | solution.py:50
  280.7 11.9 %all-to-all-start.4 = ((bf16[8,16,1536]{2,1,0:T(8,128)(2,1)}), bf16[8,16,1536]{2,1,0:T(8,128)(2,1)S(1)}, u32[]{:S(2)}, u32[]{:S(2)}) async-start(bf16[8,16,1536]{2,1,0:T(8,128)(2,1)} %add_convert_fusion.4), calls=%async_computation.4 | async-start | bytes 786432 | tf_op jit(solution)/shard_map/all_to_all | solution.py:54
  287.6 16.5 %copy-start.14 = (f32[128,1024]{1,0:T(8,128)S(1)}, f32[128,1024]{1,0:T(8,128)}, u32[]{:S(2)}) copy-start(f32[128,1024]{1,0:T(8,128)} %copy-done.13) | copy-start | bytes 1572868
  292.5 17.2 %copy-start.1 = (bf16[128,4096]{1,0:T(8,128)(2,1)S(1)}, bf16[128,4096]{1,0:T(8,128)(2,1)}, u32[]{:S(2)}) copy-start(bf16[128,4096]{1,0:T(8,128)(2,1)} %param.21) | copy-start | bytes 3145732
  292.8 7.6 %collective-permute-start.38 = (bf16[16,4224]{1,0:T(8,128)(2,1)S(1)}, bf16[16,4224]{1,0:T(8,128)(2,1)S(1)}, u32[]{:S(2)}, u32[]{:S(2)}) collective-permute-start(bf16[16,4224]{1,0:T(8,128)(2,1)S(1)} %pad_maximum_fusion.10.refs_0_), channel_id=1, source_target_pairs={{48,0},{0,16},{16,32},{32,48},{49,1},{1,17},{17,33},{33,49},{50,2}... | collective-permute-start | bytes 405512 | tf_op jit(solution)/shard_map/ppermute | solution.py:72
  293.4 8.4 %collective-permute-start.37 = (bf16[16,4224]{1,0:T(8,128)(2,1)S(1)}, bf16[16,4224]{1,0:T(8,128)(2,1)S(1)}, u32[]{:S(2)}, u32[]{:S(2)}) collective-permute-start(bf16[16,4224]{1,0:T(8,128)(2,1)S(1)} %pad_maximum_fusion.10.refs_0_), channel_id=1, source_target_pairs={{32,0},{48,16},{0,32},{16,48},{33,1},{49,17},{1,33},{17,49},{34,2}... | collective-permute-start | bytes 405512 | tf_op jit(solution)/shard_map/ppermute | solution.py:72
  295.5 8.0 %collective-permute-start.36 = (bf16[16,4224]{1,0:T(8,128)(2,1)S(1)}, bf16[16,4224]{1,0:T(8,128)(2,1)S(1)}, u32[]{:S(2)}, u32[]{:S(2)}) collective-permute-start(bf16[16,4224]{1,0:T(8,128)(2,1)S(1)} %pad_maximum_fusion.10.refs_0_), channel_id=1, source_target_pairs={{16,0},{32,16},{48,32},{0,48},{17,1},{33,17},{49,33},{1,49},{18,2}... | collective-permute-start | bytes 405512 | tf_op jit(solution)/shard_map/ppermute | solution.py:72
  296.5 9.6 %collective-permute-start.39 = (bf16[16,4224]{1,0:T(8,128)(2,1)S(1)}, bf16[16,4224]{1,0:T(8,128)(2,1)S(1)}, u32[]{:S(2)}, u32[]{:S(2)}) collective-permute-start(bf16[16,4224]{1,0:T(8,128)(2,1)S(1)} %pad_maximum_fusion.10.refs_0_), channel_id=1, source_target_pairs={{0,8},{8,0},{1,9},{9,1},{2,10},{10,2},{3,11},{11,3},{4,12},{12,4},... | collective-permute-start | bytes 405512 | tf_op jit(solution)/shard_map/ppermute | solution.py:50
  300.3 5.7 %collective-permute-start.42 = (bf16[16,4224]{1,0:T(8,128)(2,1)S(1)}, bf16[16,4224]{1,0:T(8,128)(2,1)S(1)}, u32[]{:S(2)}, u32[]{:S(2)}) collective-permute-start(bf16[16,4224]{1,0:T(8,128)(2,1)S(1)} %collective-permute-done.38.refs_3_), channel_id=1, source_target_pairs={{0,8},{8,0},{1,9},{9,1},{2,10},{10,2},{3,11},{11,3},{4,12},{12,4},... | collective-permute-start | bytes 405512 | tf_op jit(solution)/shard_map/ppermute | solution.py:50
  301.8 4.3 %collective-permute-start.41 = (bf16[16,4224]{1,0:T(8,128)(2,1)S(1)}, bf16[16,4224]{1,0:T(8,128)(2,1)S(1)}, u32[]{:S(2)}, u32[]{:S(2)}) collective-permute-start(bf16[16,4224]{1,0:T(8,128)(2,1)S(1)} %collective-permute-done.37.refs_2_), channel_id=1, source_target_pairs={{0,8},{8,0},{1,9},{9,1},{2,10},{10,2},{3,11},{11,3},{4,12},{12,4},... | collective-permute-start | bytes 405512 | tf_op jit(solution)/shard_map/ppermute | solution.py:50
  303.5 2.5 collective-permute-start.40
  (23 other events, 54.9 us)

commit v2 on v1

--- a/solution.py
+++ b/solution.py
@@ -426,7 +426,7 @@
     attended_adj, pair = lax.optimization_barrier((attended_adj, pair))
     mixed_adj = attend_backward(mixed, lse, attended_adj.reshape(length, part), scaling)
     pair = add(pick(pair, yl), pick(pair, 1 - yl), "yl")
-    mixed_adj, pair, out_sum = lax.optimization_barrier((mixed_adj, pair, out_sum))
+    mixed_adj, pair = lax.optimization_barrier((mixed_adj, pair))
     pair = add(pair, pair, "yh")
     in_weight_adj = across(hidden, mixed_adj)
     hidden_part = against(mixed_adj, in_w)

time: 315 us -> 323 us (1.025)
  waiting for transfers between devices: 111 us -> 117 us
  local copies, waits for them, and re-layouts: 22.2 us -> 26.7 us
    ppermute x15, waiting for transfers between devices: 32.6 us -> 45.9 us  [give(): return lax.ppermute(block, axis, [(i, (i + k) % n) for i in range(n)])]
    ppermute x15, waiting for transfers between devices: 35.1 us -> 30.5 us  [ahead(): return lax.ppermute(block, axis, [((i + k) % n, i) for i in range(n)])]
    unnamed x71 -> x75, local copies, waits for them, and re-layouts: 7.48 us -> 8.04 us
  transfers between devices with their start and end apart: 55 -> 55, of which waited for: 19 -> 19; matrix products, arithmetic and copies ran while one was open for 15% -> 19% of each run, Pallas kernels for 6% -> 6%
where the time goes in v2:
time: 323 us; the launch traced here: 318 us
  waiting for transfers between devices  117 us (36%)
  starting transfers between devices  93.7 us (29%)
  matrix products  29.8 us (9%)
  other arithmetic  27.1 us (8%)
  local copies, waits for them, and re-layouts  26.7 us (8%)
  Pallas kernels  21.7 us (7%)
    ppermute x15, waiting for transfers between devices, give(): return lax.ppermute(block, axis, [(i, (i + k) % n) for i in range(n)])  45.9 us
    ppermute x20, starting transfers between devices, swap(): return lax.ppermute(block, axis, SWAP)  33.9 us
    all_to_all x5, waiting for transfers between devices, trade(): return lax.all_to_all(parts, axes, split_axis=0, concat_axis=0, tiled=True)  33.2 us
    ppermute x15, waiting for transfers between devices, ahead(): return lax.ppermute(block, axis, [((i + k) % n, i) for i in range(n)])  30.5 us
    all_to_all x5, starting transfers between devices, trade(): return lax.all_to_all(parts, axes, split_axis=0, concat_axis=0, tiled=True)  23.6 us
    ppermute x15, starting transfers between devices, ahead(): return lax.ppermute(block, axis, [((i + k) % n, i) for i in range(n)])  19.6 us
    ppermute x15, starting transfers between devices, give(): return lax.ppermute(block, axis, [(i, (i + k) % n) for i in range(n)])  16.6 us
    dot_general x4, matrix products, times(): return jnp.dot(left, right, preferred_element_type=f32)  11.7 us
  transfers between devices with their start and end apart: 55, of which 19 were waited for; matrix products, arithmetic and copies ran while one was open for 19% of the time, Pallas kernels for 6%

profile of v2, /device:TPU:1, one launch (start us, length us, event | category | flops | bytes accessed | tf_op | source)
XLA Modules:
  0.0 317.8 jit_solution(16407076286353482974)
XLA Ops:
  4.8 2.1 collective-permute-start
  8.5 2.0 pad_maximum_fusion
  10.5 5.2 %collective-permute-done = bf16[192,1024]{1,0:T(8,128)(2,1)} collective-permute-done((bf16[192,1024]{1,0:T(8,128)(2,1)}, bf16[192,1024]{1,0:T(8,128)(2,1)}, u32[]{:S(2)}, u32[]{:S(2)}) %collective-permute-start) | collective-permute-done | bytes 393248 | tf_op jit(solution)/shard_map/ppermute | solution.py:50
  15.7 6.3 %all-to-all-start = ((bf16[8,184,1024]{2,1,0:T(8,128)(2,1)}), bf16[8,184,1024]{2,1,0:T(8,128)(2,1)}, u32[]{:S(2)}, u32[]{:S(2)}) async-start(bf16[8,184,1024]{2,1,0:T(8,128)(2,1)} %pad_maximum_fusion), calls=%async_computation | async-start | bytes 6029312 | tf_op jit(solution)/shard_map/all_to_all | solution.py:54
  24.8 2.4 collective-permute-start.2
  28.5 28.8 %all-to-all-done = bf16[8,184,1024]{2,1,0:T(8,128)(2,1)} async-done(((bf16[8,184,1024]{2,1,0:T(8,128)(2,1)}), bf16[8,184,1024]{2,1,0:T(8,128)(2,1)}, u32[]{:S(2)}, u32[]{:S(2)}) %all-to-all-start) | async-done | bytes 3014688 | tf_op jit(solution)/shard_map/all_to_all | solution.py:54
  58.3 1.9 convert_reduce_fusion.1
  60.3 2.3 multiply_reduce_fusion.1
  64.8 2.7 add_convert_fusion.1
  68.8 6.7 %shard_map.279 = (bf16[1024,128]{1,0:T(8,128)(2,1)S(1)}, f32[8,1024]{1,0:T(8,128)S(1)}) custom-call(bf16[1024,384]{1,0:T(8,128)(2,1)S(1)} %add_convert_fusion.3.mixed_ref), custom_call_target="tpu_custom_call" | custom-call | flops 2147483648 | bytes 1048576 | tf_op jit(solution)/shard_map/pallas_call | solution.py:262
  75.5 14.5 %collective-permute-done.2.refs_2_ = bf16[2,192,1024]{2,1,0:T(8,128)(2,1)S(1)} collective-permute-done((bf16[2,192,1024]{2,1,0:T(8,128)(2,1)S(1)}, bf16[2,192,1024]{2,1,0:T(8,128)(2,1)S(1)}, u32[]{:S(2)}, u32[]{:S(2)}) %collective-permute-start.2) | collective-permute-done | bytes 786464 | tf_op jit(solution)/shard_map/ppermute | solution.py:72
  90.1 2.7 collective-permute-start.4
  95.0 4.3 %all-to-all-start.1 = ((bf16[8,128,128]{1,2,0:T(8,128)(2,1)}), bf16[8,128,128]{1,2,0:T(8,128)(2,1)}, u32[]{:S(2)}, u32[]{:S(2)}) async-start(bf16[8,128,128]{1,2,0:T(8,128)(2,1)} %copy.48), calls=%async_computation.1 | async-start | bytes 524288 | tf_op jit(solution)/shard_map/all_to_all | solution.py:54
  100.7 2.5 collective-permute-start.12
  105.5 2.5 shard_map.280
  110.6 1.7 fusion.59
  112.8 2.3 collective-permute-start.9
  115.5 5.4 %collective-permute-done.10 = bf16[128,1024]{1,0:T(8,128)(2,1)S(1)} collective-permute-done((bf16[128,1024]{1,0:T(8,128)(2,1)S(1)}, bf16[128,1024]{1,0:T(8,128)(2,1)S(1)}, u32[]{:S(2)}, u32[]{:S(2)}) %collective-permute-start.10) | collective-permute-done | bytes 262176 | tf_op jit(solution)/shard_map/ppermute | solution.py:72
  121.1 4.8 %collective-permute-done.9 = bf16[128,1024]{1,0:T(8,128)(2,1)S(1)} collective-permute-done((bf16[128,1024]{1,0:T(8,128)(2,1)S(1)}, bf16[128,1024]{1,0:T(8,128)(2,1)S(1)}, u32[]{:S(2)}, u32[]{:S(2)}) %collective-permute-start.9) | collective-permute-done | bytes 262176 | tf_op jit(solution)/shard_map/ppermute | solution.py:72
  126.7 5.5 %multiply_convert_fusion = (bf16[512,1024]{1,0:T(8,128)(2,1)S(1)}, f32[512,1024]{1,0:T(8,128)S(1)}, f32[512,1024]{1,0:T(8,128)S(1)}) fusion(f32[1024]{0:T(1024)S(1)} %fusion.47, bf16[1024,1024]{1,0:T(8,128)(2,1)S(1)} %copy-done.9, bf16[128,1024]{1,0:T(8,128)(2,1)S(1)} %collective-permute-done.10, bf16[128,1024]{1,0:T(8,128)(2,1)S(1)} %collective-permute-done.9, ...), kind=kOutput, calls=%fused_computation.25 | convolution fusion | flops 1112539136 | bytes 8392704 | tf_op jit(solution)/shard_map/dot_general | solution.py:35
  132.3 3.0 convert_reduce_fusion.2
  138.1 4.3 %collective-permute-start.18 = (bf16[8,64,1024]{2,1,0:T(8,128)(2,1)S(1)}, bf16[8,64,1024]{2,1,0:T(8,128)(2,1)S(1)}, u32[]{:S(2)}, u32[]{:S(2)}) collective-permute-start(bf16[8,64,1024]{2,1,0:T(8,128)(2,1)S(1)} %dynamic-slice_bitcast_fusion), channel_id=1, source_target_pairs={{0,8},{8,0},{1,9},{9,1},{2,10},{10,2},{3,11},{11,3},{4,12},{12,4},... | collective-permute-start | bytes 3145736 | tf_op jit(solution)/shard_map/ppermute | solution.py:50
  142.4 2.3 convolution_convert_fusion.1
  145.0 3.0 collective-permute-start.16
  148.1 3.3 %fusion.2 = (f32[1024]{0:T(1024)S(1)}, bf16[512,1024]{1,0:T(8,128)(2,1)}) fusion(bf16[128,1024]{1,0:T(8,128)(2,1)} %collective-permute-done.13, bf16[128,1024]{1,0:T(8,128)(2,1)} %collective-permute-done.12, bf16[128,1024]{1,0:T(8,128)(2,1)S(1)} %collective-permute-done.11, bf16[128,1024]{1,0:T(8,128)(2,1)S(1)} %bitcast.263, ...), kind=kOutput, calls=%fused_computation.13 | convolution fusion | flops 1079507968 | bytes 5246976 | tf_op jit(solution)/shard_map/dot_general | solution.py:35
  151.4 3.2 %collective-permute-done.14 = bf16[128,1024]{1,0:T(8,128)(2,1)S(1)} collective-permute-done((bf16[128,1024]{1,0:T(8,128)(2,1)S(1)}, bf16[128,1024]{1,0:T(8,128)(2,1)S(1)}, u32[]{:S(2)}, u32[]{:S(2)}) %collective-permute-start.14) | collective-permute-done | bytes 262176 | tf_op jit(solution)/shard_map/ppermute | solution.py:76
  154.6 3.7 %collective-permute-done.15 = bf16[128,1024]{1,0:T(8,128)(2,1)S(1)} collective-permute-done((bf16[128,1024]{1,0:T(8,128)(2,1)S(1)}, bf16[128,1024]{1,0:T(8,128)(2,1)S(1)}, u32[]{:S(2)}, u32[]{:S(2)}) %collective-permute-start.15) | collective-permute-done | bytes 262176 | tf_op jit(solution)/shard_map/ppermute | solution.py:76
  161.3 3.0 convolution_convert_fusion.2
  165.5 2.7 collective-permute-start.19
  169.3 1.7 collective-permute-start.20
  172.7 3.7 %all-to-all-start.2 = ((bf16[8,128,128]{2,1,0:T(8,128)(2,1)}), bf16[8,128,128]{2,1,0:T(8,128)(2,1)S(1)}, u32[]{:S(2)}, u32[]{:S(2)}) async-start(bf16[8,128,128]{2,1,0:T(8,128)(2,1)} %bitcast.244), calls=%async_computation.2 | async-start | bytes 524288 | tf_op jit(solution)/shard_map/all_to_all | solution.py:54
  176.4 1.7 constant_dynamic-slice_fusion.1
  179.1 2.4 collective-permute-start.28
  181.6 12.5 %collective-permute-done.20 = bf16[2,128,1024]{2,1,0:T(8,128)(2,1)} collective-permute-done((bf16[2,128,1024]{2,1,0:T(8,128)(2,1)}, bf16[2,128,1024]{2,1,0:T(8,128)(2,1)}, u32[]{:S(2)}, u32[]{:S(2)}) %collective-permute-start.20) | collective-permute-done | bytes 524320 | tf_op jit(solution)/shard_map/ppermute | solution.py:76
  194.1 2.4 fusion.41
  198.9 7.5 %shard_map.281 = bf16[1024,384]{1,0:T(8,128)(2,1)S(1)} custom-call(bf16[1024,384]{1,0:T(8,128)(2,1)S(1)} %copy-done.11, f32[8,1024]{1,0:T(8,128)S(1)} %get-tuple-element.55.lse_ref, bf16[1024,128]{1,0:T(8,128)(2,1)S(1)} %bitcast.247), custom_call_target="tpu_custom_call" | custom-call | flops 5368709120 | bytes 2097152 | tf_op jit(solution)/shard_map/pallas_call | solution.py:278
  206.7 4.4 %fusion.55 = (bf16[1024]{0:T(1024)(128)(2,1)S(1)}, bf16[1024]{0:T(1024)(128)(2,1)S(1)}, bf16[1024,1024]{1,0:T(8,128)(2,1)}, bf16[1024,1024]{1,0:T(8,128)(2,1)S(1)}) fusion(f32[1024]{0:T(1024)S(1)} %get-tuple-element.143, f32[1024]{0:T(1024)S(1)} %get-tuple-element.141, bf16[8,184,1024]{2,1,0:T(8,128)(2,1)} %all-to-all-done, ...), kind=kOutput, calls=%fused_computation.193 | convolution fusion | flops 815790080 | bytes 7884800 | tf_op jit(solution)/shard_map/dot_general | solution.py:39
  211.1 1.9 convolution_convert_fusion.4
  213.0 2.6 collective-permute-start.23
  216.0 2.2 fusion.14
  219.8 2.3 copy.52
  222.1 1.9 dynamic-slice_bitcast_fusion.2
  224.0 4.4 %collective-permute-start.24 = (bf16[8,4,16,512]{3,2,1,0:T(8,128)(2,1)}, bf16[8,4,16,512]{3,2,1,0:T(8,128)(2,1)S(1)}, u32[]{:S(2)}, u32[]{:S(2)}) collective-permute-start(bf16[8,4,16,512]{3,2,1,0:T(8,128)(2,1)} %dynamic-slice_bitcast_fusion.2), channel_id=1, source_target_pairs={{0,8},{8,0},{1,9},{9,1},{2,10},{10,2},{3,11},{11,3},{4,12},{12,4},... | collective-permute-start | bytes 1572872 | tf_op jit(solution)/shard_map/ppermute | solution.py:50
  228.4 4.4 %all-to-all-start.3 = ((bf16[8,128,1024]{2,1,0:T(8,128)(2,1)}), bf16[8,128,1024]{2,1,0:T(8,128)(2,1)}, u32[]{:S(2)}, u32[]{:S(2)}) async-start(bf16[8,128,1024]{2,1,0:T(8,128)(2,1)} %bitcast.268), calls=%async_computation.3 | async-start | bytes 4194304 | tf_op jit(solution)/shard_map/all_to_all | solution.py:54
  233.7 3.0 collective-permute-start.44
  236.7 1.7 fusion.4
  238.6 2.9 collective-permute-start.31
  241.7 11.3 %collective-permute-done.29 = bf16[8,16,1024]{2,1,0:T(8,128)(2,1)S(1)} collective-permute-done((bf16[8,16,1024]{2,1,0:T(8,128)(2,1)S(1)}, bf16[8,16,1024]{2,1,0:T(8,128)(2,1)S(1)}, u32[]{:S(2)}, u32[]{:S(2)}) %collective-permute-start.29) | collective-permute-done | bytes 262176 | tf_op jit(solution)/shard_map/ppermute | solution.py:76
  253.1 2.6 collective-permute-start.27
  255.7 4.6 %collective-permute-done.30 = bf16[8,16,1024]{2,1,0:T(8,128)(2,1)S(1)} collective-permute-done((bf16[8,16,1024]{2,1,0:T(8,128)(2,1)S(1)}, bf16[8,16,1024]{2,1,0:T(8,128)(2,1)S(1)}, u32[]{:S(2)}, u32[]{:S(2)}) %collective-permute-start.30) | collective-permute-done | bytes 262176 | tf_op jit(solution)/shard_map/ppermute | solution.py:76
  260.4 2.8 collective-permute-done.25
  263.2 2.3 collective-permute-done.26
  265.7 4.9 %collective-permute-done.43.refs_1_ = bf16[128,1024]{1,0:T(8,128)(2,1)S(1)} collective-permute-done((bf16[128,1024]{1,0:T(8,128)(2,1)S(1)}, bf16[128,1024]{1,0:T(8,128)(2,1)S(1)}, u32[]{:S(2)}, u32[]{:S(2)}) %collective-permute-start.43) | collective-permute-done | bytes 262176 | tf_op jit(solution)/shard_map/ppermute | solution.py:72
  273.1 2.2 collective-permute-start.34
  275.3 2.6 collective-permute-start.35
  278.0 3.0 shard_map.283
  281.4 5.2 %collective-permute-done.33 = bf16[128,1024]{1,0:T(8,128)(2,1)S(1)} collective-permute-done((bf16[128,1024]{1,0:T(8,128)(2,1)S(1)}, bf16[128,1024]{1,0:T(8,128)(2,1)S(1)}, u32[]{:S(2)}, u32[]{:S(2)}) %collective-permute-start.33) | collective-permute-done | bytes 262176 | tf_op jit(solution)/shard_map/ppermute | solution.py:76
  288.3 4.9 %all-to-all-start.4 = ((bf16[8,16,1536]{2,1,0:T(8,128)(2,1)}), bf16[8,16,1536]{2,1,0:T(8,128)(2,1)S(1)}, u32[]{:S(2)}, u32[]{:S(2)}) async-start(bf16[8,16,1536]{2,1,0:T(8,128)(2,1)} %add_convert_fusion.4), calls=%async_computation.4 | async-start | bytes 786432 | tf_op jit(solution)/shard_map/all_to_all | solution.py:54
  293.2 2.0 convert_reduce_fusion
  295.8 4.4 %all-to-all-done.4 = bf16[8,16,1536]{2,1,0:T(8,128)(2,1)S(1)} async-done(((bf16[8,16,1536]{2,1,0:T(8,128)(2,1)}), bf16[8,16,1536]{2,1,0:T(8,128)(2,1)S(1)}, u32[]{:S(2)}, u32[]{:S(2)}) %all-to-all-start.4) | async-done | bytes 393248 | tf_op jit(solution)/shard_map/all_to_all | solution.py:54
  301.0 2.7 collective-permute-start.37
  304.1 4.5 %collective-permute-start.39 = (bf16[16,4224]{1,0:T(8,128)(2,1)S(1)}, bf16[16,4224]{1,0:T(8,128)(2,1)S(1)}, u32[]{:S(2)}, u32[]{:S(2)}) collective-permute-start(bf16[16,4224]{1,0:T(8,128)(2,1)S(1)} %pad_maximum_fusion.10.refs_0_), channel_id=1, source_target_pairs={{0,8},{8,0},{1,9},{9,1},{2,10},{10,2},{3,11},{11,3},{4,12},{12,4},... | collective-permute-start | bytes 405512 | tf_op jit(solution)/shard_map/ppermute | solution.py:50
  309.7 2.6 collective-permute-start.41
  313.9 2.0 shard_map.282
  (245 shorter events, 52.5 us)
Async XLA Ops:
  4.8 10.9 %collective-permute-start = (bf16[192,1024]{1,0:T(8,128)(2,1)}, bf16[192,1024]{1,0:T(8,128)(2,1)}, u32[]{:S(2)}, u32[]{:S(2)}) collective-permute-start(bf16[192,1024]{1,0:T(8,128)(2,1)} %pad_maximum_fusion.5), channel_id=1, source_target_pairs={{0,1},{1,0},{2,3},{3,2},{4,5},{5,4},{6,7},{7,6},{8,9},{9,8},{10,11... | collective-permute-start | bytes 1179656 | tf_op jit(solution)/shard_map/ppermute | solution.py:50
  15.7 41.7 %all-to-all-start = ((bf16[8,184,1024]{2,1,0:T(8,128)(2,1)}), bf16[8,184,1024]{2,1,0:T(8,128)(2,1)}, u32[]{:S(2)}, u32[]{:S(2)}) async-start(bf16[8,184,1024]{2,1,0:T(8,128)(2,1)} %pad_maximum_fusion), calls=%async_computation | async-start | bytes 6029312 | tf_op jit(solution)/shard_map/all_to_all | solution.py:54
  23.3 52.2 %collective-permute-start.3 = (bf16[2,192,1024]{2,1,0:T(8,128)(2,1)S(1)}, bf16[2,192,1024]{2,1,0:T(8,128)(2,1)S(1)}, u32[]{:S(2)}, u32[]{:S(2)}) collective-permute-start(bf16[2,192,1024]{2,1,0:T(8,128)(2,1)S(1)} %pad_maximum_fusion.4.refs_0_), channel_id=1, source_target_pairs={{6,0},{0,2},{2,4},{4,6},{7,1},{1,3},{3,5},{5,7},{14,8},{8,10},{10,... | collective-permute-start | bytes 2359304 | tf_op jit(solution)/shard_map/ppermute | solution.py:72
  24.8 65.3 %collective-permute-start.2 = (bf16[2,192,1024]{2,1,0:T(8,128)(2,1)S(1)}, bf16[2,192,1024]{2,1,0:T(8,128)(2,1)S(1)}, u32[]{:S(2)}, u32[]{:S(2)}) collective-permute-start(bf16[2,192,1024]{2,1,0:T(8,128)(2,1)S(1)} %pad_maximum_fusion.4.refs_0_), channel_id=1, source_target_pairs={{4,0},{6,2},{0,4},{2,6},{5,1},{7,3},{1,5},{3,7},{12,8},{14,10},{8,... | collective-permute-start | bytes 2359304 | tf_op jit(solution)/shard_map/ppermute | solution.py:72
  27.2 62.9 %collective-permute-start.1 = (bf16[2,192,1024]{2,1,0:T(8,128)(2,1)S(1)}, bf16[2,192,1024]{2,1,0:T(8,128)(2,1)}, u32[]{:S(2)}, u32[]{:S(2)}) collective-permute-start(bf16[2,192,1024]{2,1,0:T(8,128)(2,1)S(1)} %pad_maximum_fusion.4.refs_0_), channel_id=1, source_target_pairs={{2,0},{4,2},{6,4},{0,6},{3,1},{5,3},{7,5},{1,7},{10,8},{12,10},{14... | collective-permute-start | bytes 2359304 | tf_op jit(solution)/shard_map/ppermute | solution.py:72
  68.8 30.6 %copy-start.16 = (bf16[1,128,1024]{2,1,0:T(8,128)(2,1)S(1)}, bf16[1,128,1024]{2,1,0:T(8,128)(2,1)}, u32[]{:S(2)}) copy-start(bf16[1,128,1024]{2,1,0:T(8,128)(2,1)} %param.31) | copy-start | bytes 786436
  75.5 27.7 %copy-start.2 = (bf16[2,192,1024]{2,1,0:T(8,128)(2,1)}, bf16[2,192,1024]{2,1,0:T(8,128)(2,1)S(1)}, u32[]{:S(2)}) copy-start(bf16[2,192,1024]{2,1,0:T(8,128)(2,1)S(1)} %collective-permute-done.3.refs_3_) | copy-start | bytes 2359300
  90.1 10.6 %collective-permute-start.4 = (bf16[2,192,1024]{2,1,0:T(8,128)(2,1)S(1)}, bf16[2,192,1024]{2,1,0:T(8,128)(2,1)}, u32[]{:S(2)}, u32[]{:S(2)}) collective-permute-start(bf16[2,192,1024]{2,1,0:T(8,128)(2,1)S(1)} %pad_maximum_fusion.4.refs_0_), channel_id=1, source_target_pairs={{0,8},{8,0},{1,9},{9,1},{2,10},{10,2},{3,11},{11,3},{4,12},{12,4},... | collective-permute-start | bytes 2359304 | tf_op jit(solution)/shard_map/ppermute | solution.py:50
  92.8 10.4 %collective-permute-start.5 = (bf16[2,192,1024]{2,1,0:T(8,128)(2,1)}, bf16[2,192,1024]{2,1,0:T(8,128)(2,1)}, u32[]{:S(2)}, u32[]{:S(2)}) collective-permute-start(bf16[2,192,1024]{2,1,0:T(8,128)(2,1)} %collective-permute-done.1.refs_1_), channel_id=1, source_target_pairs={{0,8},{8,0},{1,9},{9,1},{2,10},{10,2},{3,11},{11,3},{4,12},{12,4},... | collective-permute-start | bytes 2359304 | tf_op jit(solution)/shard_map/ppermute | solution.py:50
  92.8 10.4 %collective-permute-start.6 = (bf16[2,192,1024]{2,1,0:T(8,128)(2,1)S(1)}, bf16[2,192,1024]{2,1,0:T(8,128)(2,1)}, u32[]{:S(2)}, u32[]{:S(2)}) collective-permute-start(bf16[2,192,1024]{2,1,0:T(8,128)(2,1)S(1)} %collective-permute-done.2.refs_2_), channel_id=1, source_target_pairs={{0,8},{8,0},{1,9},{9,1},{2,10},{10,2},{3,11},{11,3},{4,12},{12,4},... | collective-permute-start | bytes 2359304 | tf_op jit(solution)/shard_map/ppermute | solution.py:50
  94.2 9.0 %collective-permute-start.7 = (bf16[2,192,1024]{2,1,0:T(8,128)(2,1)S(1)}, bf16[2,192,1024]{2,1,0:T(8,128)(2,1)}, u32[]{:S(2)}, u32[]{:S(2)}) collective-permute-start(bf16[2,192,1024]{2,1,0:T(8,128)(2,1)S(1)} %collective-permute-done.3.refs_3_), channel_id=1, source_target_pairs={{0,8},{8,0},{1,9},{9,1},{2,10},{10,2},{3,11},{11,3},{4,12},{12,4},... | collective-permute-start | bytes 2359304 | tf_op jit(solution)/shard_map/ppermute | solution.py:50
  95.0 15.6 %all-to-all-start.1 = ((bf16[8,128,128]{1,2,0:T(8,128)(2,1)}), bf16[8,128,128]{1,2,0:T(8,128)(2,1)}, u32[]{:S(2)}, u32[]{:S(2)}) async-start(bf16[8,128,128]{1,2,0:T(8,128)(2,1)} %copy.48), calls=%async_computation.1 | async-start | bytes 524288 | tf_op jit(solution)/shard_map/all_to_all | solution.py:54
  99.3 32.9 %collective-permute-start.13 = (bf16[128,1024]{1,0:T(8,128)(2,1)S(1)}, bf16[128,1024]{1,0:T(8,128)(2,1)}, u32[]{:S(2)}, u32[]{:S(2)}) collective-permute-start(bf16[128,1024]{1,0:T(8,128)(2,1)S(1)} %bitcast.258), channel_id=1, source_target_pairs={{48,0},{0,16},{16,32},{32,48},{49,1},{1,17},{17,33},{33,49},{50,2}... | collective-permute-start | bytes 786440 | tf_op jit(solution)/shard_map/ppermute | solution.py:72
  100.7 31.6 %collective-permute-start.12 = (bf16[128,1024]{1,0:T(8,128)(2,1)S(1)}, bf16[128,1024]{1,0:T(8,128)(2,1)}, u32[]{:S(2)}, u32[]{:S(2)}) collective-permute-start(bf16[128,1024]{1,0:T(8,128)(2,1)S(1)} %bitcast.259), channel_id=1, source_target_pairs={{32,0},{48,16},{0,32},{16,48},{33,1},{49,17},{1,33},{17,49},{34,2}... | collective-permute-start | bytes 786440 | tf_op jit(solution)/shard_map/ppermute | solution.py:72
  110.6 16.1 %copy-start.9 = (bf16[1024,1024]{1,0:T(8,128)(2,1)S(1)}, bf16[1024,1024]{1,0:T(8,128)(2,1)}, u32[]{:S(2)}) copy-start(bf16[1024,1024]{1,0:T(8,128)(2,1)} %copy-done.8) | copy-start | bytes 6291460
  112.7 8.2 %collective-permute-start.10 = (bf16[128,1024]{1,0:T(8,128)(2,1)S(1)}, bf16[128,1024]{1,0:T(8,128)(2,1)S(1)}, u32[]{:S(2)}, u32[]{:S(2)}) collective-permute-start(bf16[128,1024]{1,0:T(8,128)(2,1)S(1)} %add_convert_fusion.7), channel_id=1, source_target_pairs={{48,0},{0,16},{16,32},{32,48},{49,1},{1,17},{17,33},{33,49},{50,2}... | collective-permute-start | bytes 786440 | tf_op jit(solution)/shard_map/ppermute | solution.py:72
  112.8 13.1 %collective-permute-start.9 = (bf16[128,1024]{1,0:T(8,128)(2,1)S(1)}, bf16[128,1024]{1,0:T(8,128)(2,1)S(1)}, u32[]{:S(2)}, u32[]{:S(2)}) collective-permute-start(bf16[128,1024]{1,0:T(8,128)(2,1)S(1)} %add_convert_fusion.7), channel_id=1, source_target_pairs={{32,0},{48,16},{0,32},{16,48},{33,1},{49,17},{1,33},{17,49},{34,2}... | collective-permute-start | bytes 786440 | tf_op jit(solution)/shard_map/ppermute | solution.py:72
  115.1 11.6 %collective-permute-start.8 = (bf16[128,1024]{1,0:T(8,128)(2,1)S(1)}, bf16[128,1024]{1,0:T(8,128)(2,1)S(1)}, u32[]{:S(2)}, u32[]{:S(2)}) collective-permute-start(bf16[128,1024]{1,0:T(8,128)(2,1)S(1)} %add_convert_fusion.7), channel_id=1, source_target_pairs={{16,0},{32,16},{48,32},{0,48},{17,1},{33,17},{49,33},{1,49},{18,2}... | collective-permute-start | bytes 786440 | tf_op jit(solution)/shard_map/ppermute | solution.py:72
  120.8 11.4 %collective-permute-start.11 = (bf16[128,1024]{1,0:T(8,128)(2,1)S(1)}, bf16[128,1024]{1,0:T(8,128)(2,1)S(1)}, u32[]{:S(2)}, u32[]{:S(2)}) collective-permute-start(bf16[128,1024]{1,0:T(8,128)(2,1)S(1)} %bitcast.260), channel_id=1, source_target_pairs={{16,0},{32,16},{48,32},{0,48},{17,1},{33,17},{49,33},{1,49},{18,2}... | collective-permute-start | bytes 786440 | tf_op jit(solution)/shard_map/ppermute | solution.py:72
  138.1 20.4 %collective-permute-start.18 = (bf16[8,64,1024]{2,1,0:T(8,128)(2,1)S(1)}, bf16[8,64,1024]{2,1,0:T(8,128)(2,1)S(1)}, u32[]{:S(2)}, u32[]{:S(2)}) collective-permute-start(bf16[8,64,1024]{2,1,0:T(8,128)(2,1)S(1)} %dynamic-slice_bitcast_fusion), channel_id=1, source_target_pairs={{0,8},{8,0},{1,9},{9,1},{2,10},{10,2},{3,11},{11,3},{4,12},{12,4},... | collective-permute-start | bytes 3145736 | tf_op jit(solution)/shard_map/ppermute | solution.py:50
  144.8 14.1 %collective-permute-start.17 = (bf16[8,64,1024]{2,1,0:T(8,128)(2,1)S(1)}, bf16[8,64,1024]{2,1,0:T(8,128)(2,1)S(1)}, u32[]{:S(2)}, u32[]{:S(2)}) collective-permute-start(bf16[8,64,1024]{2,1,0:T(8,128)(2,1)S(1)} %dynamic-slice_bitcast_fusion.1), channel_id=1, source_target_pairs={{0,8},{8,0},{1,9},{9,1},{2,10},{10,2},{3,11},{11,3},{4,12},{12,4},... | collective-permute-start | bytes 3145736 | tf_op jit(solution)/shard_map/ppermute | solution.py:50
  145.0 9.6 %collective-permute-start.14 = (bf16[128,1024]{1,0:T(8,128)(2,1)S(1)}, bf16[128,1024]{1,0:T(8,128)(2,1)S(1)}, u32[]{:S(2)}, u32[]{:S(2)}) collective-permute-start(bf16[128,1024]{1,0:T(8,128)(2,1)S(1)} %get-tuple-element.106), channel_id=1, source_target_pairs={{0,16},{16,32},{32,48},{48,0},{1,17},{17,33},{33,49},{49,1},{2,18}... | collective-permute-start | bytes 786440 | tf_op jit(solution)/shard_map/ppermute | solution.py:76
  145.0 9.5 %collective-permute-start.16 = (bf16[128,1024]{1,0:T(8,128)(2,1)S(1)}, bf16[128,1024]{1,0:T(8,128)(2,1)S(1)}, u32[]{:S(2)}, u32[]{:S(2)}) collective-permute-start(bf16[128,1024]{1,0:T(8,128)(2,1)S(1)} %get-tuple-element.107), channel_id=1, source_target_pairs={{0,48},{16,0},{32,16},{48,32},{1,49},{17,1},{33,17},{49,33},{2,50}... | collective-permute-start | bytes 786440 | tf_op jit(solution)/shard_map/ppermute | solution.py:76
  148.1 10.2 %collective-permute-start.15 = (bf16[128,1024]{1,0:T(8,128)(2,1)S(1)}, bf16[128,1024]{1,0:T(8,128)(2,1)S(1)}, u32[]{:S(2)}, u32[]{:S(2)}) collective-permute-start(bf16[128,1024]{1,0:T(8,128)(2,1)S(1)} %get-tuple-element.108), channel_id=1, source_target_pairs={{0,32},{16,48},{32,0},{48,16},{1,33},{17,49},{33,1},{49,17},{2,34}... | collective-permute-start | bytes 786440 | tf_op jit(solution)/shard_map/ppermute | solution.py:76
  165.5 16.1 %collective-permute-start.19 = (bf16[2,128,1024]{2,1,0:T(8,128)(2,1)}, bf16[2,128,1024]{2,1,0:T(8,128)(2,1)}, u32[]{:S(2)}, u32[]{:S(2)}) collective-permute-start(bf16[2,128,1024]{2,1,0:T(8,128)(2,1)} %get-tuple-element.95), channel_id=1, source_target_pairs={{0,2},{2,4},{4,6},{6,0},{1,3},{3,5},{5,7},{7,1},{8,10},{10,12},{12... | collective-permute-start | bytes 1572872 | tf_op jit(solution)/shard_map/ppermute | solution.py:76
  168.2 13.4 %collective-permute-start.21 = (bf16[2,128,1024]{2,1,0:T(8,128)(2,1)}, bf16[2,128,1024]{2,1,0:T(8,128)(2,1)}, u32[]{:S(2)}, u32[]{:S(2)}) collective-permute-start(bf16[2,128,1024]{2,1,0:T(8,128)(2,1)} %get-tuple-element.96), channel_id=1, source_target_pairs={{0,6},{2,0},{4,2},{6,4},{1,7},{3,1},{5,3},{7,5},{8,14},{10,8},{12,... | collective-permute-start | bytes 1572872 | tf_op jit(solution)/shard_map/ppermute | solution.py:76
  169.3 24.8 %collective-permute-start.20 = (bf16[2,128,1024]{2,1,0:T(8,128)(2,1)}, bf16[2,128,1024]{2,1,0:T(8,128)(2,1)}, u32[]{:S(2)}, u32[]{:S(2)}) collective-permute-start(bf16[2,128,1024]{2,1,0:T(8,128)(2,1)} %get-tuple-element.97), channel_id=1, source_target_pairs={{0,4},{2,6},{4,0},{6,2},{1,5},{3,7},{5,1},{7,3},{8,12},{10,14},{12... | collective-permute-start | bytes 1572872 | tf_op jit(solution)/shard_map/ppermute | solution.py:76
  172.7 23.8 %all-to-all-start.2 = ((bf16[8,128,128]{2,1,0:T(8,128)(2,1)}), bf16[8,128,128]{2,1,0:T(8,128)(2,1)S(1)}, u32[]{:S(2)}, u32[]{:S(2)}) async-start(bf16[8,128,128]{2,1,0:T(8,128)(2,1)} %bitcast.244), calls=%async_computation.2 | async-start | bytes 524288 | tf_op jit(solution)/shard_map/all_to_all | solution.py:54
  179.1 19.8 %copy-start.11 = (bf16[1024,384]{1,0:T(8,128)(2,1)S(1)}, bf16[1024,384]{1,0:T(8,128)(2,1)}, u32[]{:S(2)}) copy-start(bf16[1024,384]{1,0:T(8,128)(2,1)} %copy-done.10) | copy-start | bytes 2359300
  179.1 57.6 %collective-permute-start.28 = (bf16[8,4,16,1024]{3,2,0,1:T(8,128)(2,1)}, bf16[8,4,16,1024]{3,2,0,1:T(8,128)(2,1)}, u32[]{:S(2)}, u32[]{:S(2)}) collective-permute-start(bf16[8,4,16,1024]{3,2,0,1:T(8,128)(2,1)} %bitcast.242), channel_id=1, source_target_pairs={{0,8},{8,0},{1,9},{9,1},{2,10},{10,2},{3,11},{11,3},{4,12},{12,4},... | collective-permute-start | bytes 3145736 | tf_op jit(solution)/shard_map/ppermute | solution.py:50
  197.5 9.0 %collective-permute-start.22 = (bf16[128,1024]{1,0:T(8,128)(2,1)S(1)}, bf16[128,1024]{1,0:T(8,128)(2,1)S(1)}, u32[]{:S(2)}, u32[]{:S(2)}) collective-permute-start(bf16[128,1024]{1,0:T(8,128)(2,1)S(1)} %dynamic-slice_bitcast_fusion.9), channel_id=1, source_target_pairs={{0,1},{1,0},{2,3},{3,2},{4,5},{5,4},{6,7},{7,6},{8,9},{9,8},{10,11... | collective-permute-start | bytes 786440 | tf_op jit(solution)/shard_map/ppermute | solution.py:50
  198.9 7.6 %copy-start.18 = (bf16[2,128,1024]{2,1,0:T(8,128)(2,1)S(1)}, bf16[2,128,1024]{2,1,0:T(8,128)(2,1)}, u32[]{:S(2)}) copy-start(bf16[2,128,1024]{2,1,0:T(8,128)(2,1)} %fusion.41) | copy-start | bytes 1572868
  198.9 7.8 %copy-start.20 = (bf16[8,8,16,3,128]{4,3,2,1,0:T(4,128)(2,1)S(1)}, bf16[8,8,16,3,128]{4,3,2,1,0:T(4,128)(2,1)}, u32[]{:S(2)}) copy-start(bf16[8,8,16,3,128]{4,3,2,1,0:T(4,128)(2,1)} %copy-done.19) | copy-start | bytes 2359300
  213.0 6.7 %collective-permute-start.23 = (bf16[128,1024]{1,0:T(8,128)(2,1)S(1)}, bf16[128,1024]{1,0:T(8,128)(2,1)S(1)}, u32[]{:S(2)}, u32[]{:S(2)}) collective-permute-start(bf16[128,1024]{1,0:T(8,128)(2,1)S(1)} %fusion.39), channel_id=1, source_target_pairs={{0,64},{64,0},{1,65},{65,1},{2,66},{66,2},{3,67},{67,3},{4,68},{68... | collective-permute-start | bytes 786440 | tf_op jit(solution)/shard_map/ppermute | solution.py:50
  224.0 17.5 %collective-permute-start.24 = (bf16[8,4,16,512]{3,2,1,0:T(8,128)(2,1)}, bf16[8,4,16,512]{3,2,1,0:T(8,128)(2,1)S(1)}, u32[]{:S(2)}, u32[]{:S(2)}) collective-permute-start(bf16[8,4,16,512]{3,2,1,0:T(8,128)(2,1)} %dynamic-slice_bitcast_fusion.2), channel_id=1, source_target_pairs={{0,8},{8,0},{1,9},{9,1},{2,10},{10,2},{3,11},{11,3},{4,12},{12,4},... | collective-permute-start | bytes 1572872 | tf_op jit(solution)/shard_map/ppermute | solution.py:50
  228.4 59.9 %all-to-all-start.3 = ((bf16[8,128,1024]{2,1,0:T(8,128)(2,1)}), bf16[8,128,1024]{2,1,0:T(8,128)(2,1)}, u32[]{:S(2)}, u32[]{:S(2)}) async-start(bf16[8,128,1024]{2,1,0:T(8,128)(2,1)} %bitcast.268), calls=%async_computation.3 | async-start | bytes 4194304 | tf_op jit(solution)/shard_map/all_to_all | solution.py:54
  232.7 32.9 %collective-permute-start.45 = (bf16[128,1024]{1,0:T(8,128)(2,1)S(1)}, bf16[128,1024]{1,0:T(8,128)(2,1)S(1)}, u32[]{:S(2)}, u32[]{:S(2)}) collective-permute-start(bf16[128,1024]{1,0:T(8,128)(2,1)S(1)} %add_convert_fusion.6.refs_0_), channel_id=1, source_target_pairs={{48,0},{0,16},{16,32},{32,48},{49,1},{1,17},{17,33},{33,49},{50,2}... | collective-permute-start | bytes 786440 | tf_op jit(solution)/shard_map/ppermute | solution.py:72
  233.7 31.9 %collective-permute-start.44 = (bf16[128,1024]{1,0:T(8,128)(2,1)S(1)}, bf16[128,1024]{1,0:T(8,128)(2,1)S(1)}, u32[]{:S(2)}, u32[]{:S(2)}) collective-permute-start(bf16[128,1024]{1,0:T(8,128)(2,1)S(1)} %add_convert_fusion.6.refs_0_), channel_id=1, source_target_pairs={{32,0},{48,16},{0,32},{16,48},{33,1},{49,17},{1,33},{17,49},{34,2}... | collective-permute-start | bytes 786440 | tf_op jit(solution)/shard_map/ppermute | solution.py:72
  238.5 14.5 %collective-permute-start.29 = (bf16[8,16,1024]{2,1,0:T(8,128)(2,1)S(1)}, bf16[8,16,1024]{2,1,0:T(8,128)(2,1)S(1)}, u32[]{:S(2)}, u32[]{:S(2)}) collective-permute-start(bf16[8,16,1024]{2,1,0:T(8,128)(2,1)S(1)} %get-tuple-element.103), channel_id=1, source_target_pairs={{0,16},{16,32},{32,48},{48,0},{1,17},{17,33},{33,49},{49,1},{2,18}... | collective-permute-start | bytes 786440 | tf_op jit(solution)/shard_map/ppermute | solution.py:76
  238.6 14.5 %collective-permute-start.31 = (bf16[8,16,1024]{2,1,0:T(8,128)(2,1)S(1)}, bf16[8,16,1024]{2,1,0:T(8,128)(2,1)S(1)}, u32[]{:S(2)}, u32[]{:S(2)}) collective-permute-start(bf16[8,16,1024]{2,1,0:T(8,128)(2,1)S(1)} %get-tuple-element.104), channel_id=1, source_target_pairs={{0,48},{16,0},{32,16},{48,32},{1,49},{17,1},{33,17},{49,33},{2,50}... | collective-permute-start | bytes 786440 | tf_op jit(solution)/shard_map/ppermute | solution.py:76
  241.4 18.8 %collective-permute-start.30 = (bf16[8,16,1024]{2,1,0:T(8,128)(2,1)S(1)}, bf16[8,16,1024]{2,1,0:T(8,128)(2,1)S(1)}, u32[]{:S(2)}, u32[]{:S(2)}) collective-permute-start(bf16[8,16,1024]{2,1,0:T(8,128)(2,1)S(1)} %get-tuple-element.105), channel_id=1, source_target_pairs={{0,32},{16,48},{32,0},{48,16},{1,33},{17,49},{33,1},{49,17},{2,34}... | collective-permute-start | bytes 786440 | tf_op jit(solution)/shard_map/ppermute | solution.py:76
  241.7 30.8 %copy-start.21 = (bf16[512,1024]{1,0:T(8,128)(2,1)S(1)}, bf16[512,1024]{1,0:T(8,128)(2,1)}, u32[]{:S(2)}) copy-start(bf16[512,1024]{1,0:T(8,128)(2,1)} %get-tuple-element.94) | copy-start | bytes 3145732
  253.0 10.2 %collective-permute-start.25 = (bf16[8,16,512]{2,1,0:T(8,128)(2,1)S(1)}, bf16[8,16,512]{2,1,0:T(8,128)(2,1)S(1)}, u32[]{:S(2)}, u32[]{:S(2)}) collective-permute-start(bf16[8,16,512]{2,1,0:T(8,128)(2,1)S(1)} %get-tuple-element.111), channel_id=1, source_target_pairs={{0,16},{16,32},{32,48},{48,0},{1,17},{17,33},{33,49},{49,1},{2,18}... | collective-permute-start | bytes 393224 | tf_op jit(solution)/shard_map/ppermute | solution.py:76
  253.1 10.1 %collective-permute-start.27 = (bf16[8,16,512]{2,1,0:T(8,128)(2,1)S(1)}, bf16[8,16,512]{2,1,0:T(8,128)(2,1)S(1)}, u32[]{:S(2)}, u32[]{:S(2)}) collective-permute-start(bf16[8,16,512]{2,1,0:T(8,128)(2,1)S(1)} %get-tuple-element.112), channel_id=1, source_target_pairs={{0,48},{16,0},{32,16},{48,32},{1,49},{17,1},{33,17},{49,33},{2,50}... | collective-permute-start | bytes 393224 | tf_op jit(solution)/shard_map/ppermute | solution.py:76
  260.2 5.3 %collective-permute-start.26 = (bf16[8,16,512]{2,1,0:T(8,128)(2,1)S(1)}, bf16[8,16,512]{2,1,0:T(8,128)(2,1)S(1)}, u32[]{:S(2)}, u32[]{:S(2)}) collective-permute-start(bf16[8,16,512]{2,1,0:T(8,128)(2,1)S(1)} %get-tuple-element.113), channel_id=1, source_target_pairs={{0,32},{16,48},{32,0},{48,16},{1,33},{17,49},{33,1},{49,17},{2,34}... | collective-permute-start | bytes 393224 | tf_op jit(solution)/shard_map/ppermute | solution.py:76
  263.2 7.4 %collective-permute-start.43 = (bf16[128,1024]{1,0:T(8,128)(2,1)S(1)}, bf16[128,1024]{1,0:T(8,128)(2,1)S(1)}, u32[]{:S(2)}, u32[]{:S(2)}) collective-permute-start(bf16[128,1024]{1,0:T(8,128)(2,1)S(1)} %add_convert_fusion.6.refs_0_), channel_id=1, source_target_pairs={{16,0},{32,16},{48,32},{0,48},{17,1},{33,17},{49,33},{1,49},{18,2}... | collective-permute-start | bytes 786440 | tf_op jit(solution)/shard_map/ppermute | solution.py:72
  270.6 2.5 collective-permute-start.46
  271.9 3.3 %collective-permute-start.47 = (bf16[128,1024]{1,0:T(8,128)(2,1)S(1)}, bf16[128,1024]{1,0:T(8,128)(2,1)S(1)}, u32[]{:S(2)}, u32[]{:S(2)}) collective-permute-start(bf16[128,1024]{1,0:T(8,128)(2,1)S(1)} %collective-permute-done.43.refs_1_), channel_id=1, source_target_pairs={{0,8},{8,0},{1,9},{9,1},{2,10},{10,2},{3,11},{11,3},{4,12},{12,4},... | collective-permute-start | bytes 786440 | tf_op jit(solution)/shard_map/ppermute | solution.py:50
  271.9 3.4 %collective-permute-start.48 = (bf16[128,1024]{1,0:T(8,128)(2,1)S(1)}, bf16[128,1024]{1,0:T(8,128)(2,1)S(1)}, u32[]{:S(2)}, u32[]{:S(2)}) collective-permute-start(bf16[128,1024]{1,0:T(8,128)(2,1)S(1)} %collective-permute-done.44.refs_2_), channel_id=1, source_target_pairs={{0,8},{8,0},{1,9},{9,1},{2,10},{10,2},{3,11},{11,3},{4,12},{12,4},... | collective-permute-start | bytes 786440 | tf_op jit(solution)/shard_map/ppermute | solution.py:50
  272.4 5.5 %collective-permute-start.49 = (bf16[128,1024]{1,0:T(8,128)(2,1)S(1)}, bf16[128,1024]{1,0:T(8,128)(2,1)S(1)}, u32[]{:S(2)}, u32[]{:S(2)}) collective-permute-start(bf16[128,1024]{1,0:T(8,128)(2,1)S(1)} %collective-permute-done.45.refs_3_), channel_id=1, source_target_pairs={{0,8},{8,0},{1,9},{9,1},{2,10},{10,2},{3,11},{11,3},{4,12},{12,4},... | collective-permute-start | bytes 786440 | tf_op jit(solution)/shard_map/ppermute | solution.py:50
  272.5 8.9 %collective-permute-start.32 = (bf16[128,1024]{1,0:T(8,128)(2,1)S(1)}, bf16[128,1024]{1,0:T(8,128)(2,1)S(1)}, u32[]{:S(2)}, u32[]{:S(2)}) collective-permute-start(bf16[128,1024]{1,0:T(8,128)(2,1)S(1)} %get-tuple-element.100), channel_id=1, source_target_pairs={{0,16},{16,32},{32,48},{48,0},{1,17},{17,33},{33,49},{49,1},{2,18}... | collective-permute-start | bytes 786440 | tf_op jit(solution)/shard_map/ppermute | solution.py:76
  273.1 8.3 %collective-permute-start.34 = (bf16[128,1024]{1,0:T(8,128)(2,1)S(1)}, bf16[128,1024]{1,0:T(8,128)(2,1)S(1)}, u32[]{:S(2)}, u32[]{:S(2)}) collective-permute-start(bf16[128,1024]{1,0:T(8,128)(2,1)S(1)} %get-tuple-element.101), channel_id=1, source_target_pairs={{0,48},{16,0},{32,16},{48,32},{1,49},{17,1},{33,17},{49,33},{2,50}... | collective-permute-start | bytes 786440 | tf_op jit(solution)/shard_map/ppermute | solution.py:76
  275.2 11.3 %collective-permute-start.33 = (bf16[128,1024]{1,0:T(8,128)(2,1)S(1)}, bf16[128,1024]{1,0:T(8,128)(2,1)S(1)}, u32[]{:S(2)}, u32[]{:S(2)}) collective-permute-start(bf16[128,1024]{1,0:T(8,128)(2,1)S(1)} %get-tuple-element.102), channel_id=1, source_target_pairs={{0,32},{16,48},{32,0},{48,16},{1,33},{17,49},{33,1},{49,17},{2,34}... | collective-permute-start | bytes 786440 | tf_op jit(solution)/shard_map/ppermute | solution.py:76
  275.3 12.2 %collective-permute-start.35 = (bf16[8,16,1536]{2,1,0:T(8,128)(2,1)S(1)}, bf16[8,16,1536]{2,1,0:T(8,128)(2,1)S(1)}, u32[]{:S(2)}, u32[]{:S(2)}) collective-permute-start(bf16[8,16,1536]{2,1,0:T(8,128)(2,1)S(1)} %pad_maximum_fusion.6), channel_id=1, source_target_pairs={{0,64},{64,0},{1,65},{65,1},{2,66},{66,2},{3,67},{67,3},{4,68},{68... | collective-permute-start | bytes 1179656 | tf_op jit(solution)/shard_map/ppermute | solution.py:50
  287.4 7.8 %copy-start.14 = (bf16[1,128,1024]{2,1,0:T(8,128)(2,1)S(1)}, bf16[1,128,1024]{2,1,0:T(8,128)(2,1)}, u32[]{:S(2)}) copy-start(bf16[1,128,1024]{2,1,0:T(8,128)(2,1)} %param.16) | copy-start | bytes 786436
  288.3 11.9 %all-to-all-start.4 = ((bf16[8,16,1536]{2,1,0:T(8,128)(2,1)}), bf16[8,16,1536]{2,1,0:T(8,128)(2,1)S(1)}, u32[]{:S(2)}, u32[]{:S(2)}) async-start(bf16[8,16,1536]{2,1,0:T(8,128)(2,1)} %add_convert_fusion.4), calls=%async_computation.4 | async-start | bytes 786432 | tf_op jit(solution)/shard_map/all_to_all | solution.py:54
  300.2 17.4 %copy-start.1 = (bf16[128,4096]{1,0:T(8,128)(2,1)S(1)}, bf16[128,4096]{1,0:T(8,128)(2,1)}, u32[]{:S(2)}) copy-start(bf16[128,4096]{1,0:T(8,128)(2,1)} %param.21) | copy-start | bytes 3145732
  300.4 8.2 %collective-permute-start.38 = (bf16[16,4224]{1,0:T(8,128)(2,1)S(1)}, bf16[16,4224]{1,0:T(8,128)(2,1)S(1)}, u32[]{:S(2)}, u32[]{:S(2)}) collective-permute-start(bf16[16,4224]{1,0:T(8,128)(2,1)S(1)} %pad_maximum_fusion.10.refs_0_), channel_id=1, source_target_pairs={{48,0},{0,16},{16,32},{32,48},{49,1},{1,17},{17,33},{33,49},{50,2}... | collective-permute-start | bytes 405512 | tf_op jit(solution)/shard_map/ppermute | solution.py:72
  301.0 8.7 %collective-permute-start.37 = (bf16[16,4224]{1,0:T(8,128)(2,1)S(1)}, bf16[16,4224]{1,0:T(8,128)(2,1)S(1)}, u32[]{:S(2)}, u32[]{:S(2)}) collective-permute-start(bf16[16,4224]{1,0:T(8,128)(2,1)S(1)} %pad_maximum_fusion.10.refs_0_), channel_id=1, source_target_pairs={{32,0},{48,16},{0,32},{16,48},{33,1},{49,17},{1,33},{17,49},{34,2}... | collective-permute-start | bytes 405512 | tf_op jit(solution)/shard_map/ppermute | solution.py:72
  303.7 8.6 %collective-permute-start.36 = (bf16[16,4224]{1,0:T(8,128)(2,1)S(1)}, bf16[16,4224]{1,0:T(8,128)(2,1)S(1)}, u32[]{:S(2)}, u32[]{:S(2)}) collective-permute-start(bf16[16,4224]{1,0:T(8,128)(2,1)S(1)} %pad_maximum_fusion.10.refs_0_), channel_id=1, source_target_pairs={{16,0},{32,16},{48,32},{0,48},{17,1},{33,17},{49,33},{1,49},{18,2}... | collective-permute-start | bytes 405512 | tf_op jit(solution)/shard_map/ppermute | solution.py:72
  304.1 9.8 %collective-permute-start.39 = (bf16[16,4224]{1,0:T(8,128)(2,1)S(1)}, bf16[16,4224]{1,0:T(8,128)(2,1)S(1)}, u32[]{:S(2)}, u32[]{:S(2)}) collective-permute-start(bf16[16,4224]{1,0:T(8,128)(2,1)S(1)} %pad_maximum_fusion.10.refs_0_), channel_id=1, source_target_pairs={{0,8},{8,0},{1,9},{9,1},{2,10},{10,2},{3,11},{11,3},{4,12},{12,4},... | collective-permute-start | bytes 405512 | tf_op jit(solution)/shard_map/ppermute | solution.py:50
  308.6 5.2 %collective-permute-start.42 = (bf16[16,4224]{1,0:T(8,128)(2,1)S(1)}, bf16[16,4224]{1,0:T(8,128)(2,1)S(1)}, u32[]{:S(2)}, u32[]{:S(2)}) collective-permute-start(bf16[16,4224]{1,0:T(8,128)(2,1)S(1)} %collective-permute-done.38.refs_3_), channel_id=1, source_target_pairs={{0,8},{8,0},{1,9},{9,1},{2,10},{10,2},{3,11},{11,3},{4,12},{12,4},... | collective-permute-start | bytes 405512 | tf_op jit(solution)/shard_map/ppermute | solution.py:50
  309.7 4.1 %collective-permute-start.41 = (bf16[16,4224]{1,0:T(8,128)(2,1)S(1)}, bf16[16,4224]{1,0:T(8,128)(2,1)S(1)}, u32[]{:S(2)}, u32[]{:S(2)}) collective-permute-start(bf16[16,4224]{1,0:T(8,128)(2,1)S(1)} %collective-permute-done.37.refs_2_), channel_id=1, source_target_pairs={{0,8},{8,0},{1,9},{9,1},{2,10},{10,2},{3,11},{11,3},{4,12},{12,4},... | collective-permute-start | bytes 405512 | tf_op jit(solution)/shard_map/ppermute | solution.py:50
  312.3 1.6 collective-permute-start.40
  (25 other events, 63.9 us)
